TPU v7x, 32 devices: a whole 2x2x4 slice. The times are simulated.
32 devices in a mesh: gx: 4 (over y, x), gy: 8 (over z, core).
Axes of the slice: x: 2, y: 2, z: 4, core: 2. Of those that a mesh axis runs over, the one named last changes fastest.
Arguments:
- voxel_feats: bfloat16 [128, 64, 128], P(('gx', 'gy')), may hold values from -6 to 6
- w_first: bfloat16 [27, 128, 128], replicated, may hold values from -0.109375 to 0.109375
- w_second: bfloat16 [27, 128, 128], replicated, may hold values from -0.109375 to 0.109375
- norm_gain: float32 [2, 128], replicated, may hold values from 0.5 to 1.5
- norm_shift: float32 [2, 128], replicated, may hold values from -3 to 3
- grad_out: bfloat16 [128, 64, 128], P(('gx', 'gy')), may hold values from -6 to 6
- brick_count: int32 [32], P(('gx', 'gy')), may hold values from 1 to 4, as said below
- kernel_map: int32 [128, 27], P(('gx', 'gy')), may hold values from 0 to 12, as said below
- face_send: int32 [32, 4, 1], P(('gx', 'gy')), may hold values from 0 to 3, as said below
- corner_send: int32 [32, 4, 1], P(('gx', 'gy')), may hold values from 0 to 3, as said below
Outputs:
- out_feats: bfloat16 [128, 64, 128], P(('gx', 'gy'))
- grad_in: bfloat16 [128, 64, 128], P(('gx', 'gy'))
- weight_grads: float32 [2, 27, 128, 128], replicated
- norm_grads: float32 [4, 128], replicated
Inputs may be any that keep to these rules, and one draw needn't show every extreme that they name: `brick_count`: some tile is full in every draw. `kernel_map`: direction 13 names the brick itself; index 12 is the zero brick. `face_send`: list k names bricks of the tile below its brick_count, sent to its +x, -x, +y, -y neighbour for k = 0, 1, 2, 3. `corner_send`: list k names bricks of the tile below its brick_count, sent to its (+x, +y), (+x, -y), (-x, +y), (-x, -y) neighbour for k = 0, 1, 2, 3.
All inputs are finite; a program needn't handle non-finite values.
Results may differ from a plain program's by a relative error of at most 0.006.
Values may be sent and summed in bfloat16 or wider, within the bound.
A program may use at most 128 MiB of HBM per device.

v0:
```python
import jax
import jax.numpy as jnp
from jax import lax
from jax.sharding import PartitionSpec as P

TAP_LIST = [(a, b, c) for a in range(3) for b in range(3) for c in range(3)]
epsilon = 1e-05


def shifted(value, axis, by):
    length = lax.axis_size(axis)
    pairs = [(i, i + by) for i in range(length) if 0 <= i + by < length]
    return lax.ppermute(value, axis, pairs)


def silu_slope(values):
    sigma = jax.nn.sigmoid(values)
    return sigma * (1.0 + values * (1.0 - sigma))


def source_range(e):
    if e < 0:
        return (slice(3, 4), slice(0, 1))
    if e == 0:
        return (slice(0, 4), slice(1, 5))
    return (slice(0, 1), slice(5, 6))


def assemble(extended, tile_table):
    planes = []
    for a in (-1, 0, 1):
        layers = []
        for b in (-1, 0, 1):
            pieces = []
            for c in (-1, 0, 1):
                d = 9 * (a + 1) + 3 * (b + 1) + (c + 1)
                region = extended[:, source_range(a)[0], source_range(b)[0], source_range(c)[0]]
                pieces.append(jnp.take(region, tile_table[:, d], axis=0))
            layers.append(jnp.concatenate(pieces, axis=3))
        planes.append(jnp.concatenate(layers, axis=2))
    return jnp.concatenate(planes, axis=1)


def patches(padded):
    bricks = padded.shape[0]
    channels = padded.shape[-1]
    return jnp.concatenate(
        [
            padded[:, a : a + 4, b : b + 4, c : c + 4].reshape(bricks * 64, channels)
            for a, b, c in TAP_LIST
        ],
        axis=1,
    )


def spread(columns, bricks, channels):
    padded = jnp.zeros((bricks, 6, 6, 6, channels), jnp.float32)
    for k, (a, b, c) in enumerate(TAP_LIST):
        piece = columns[:, k * channels : (k + 1) * channels].reshape(bricks, 4, 4, 4, channels)
        padded = padded.at[:, a : a + 4, b : b + 4, c : c + 4].add(piece)
    return padded


def scatter_bricks(padded, tile_table, total):
    result = jnp.zeros((total, 4, 4, 4, padded.shape[-1]), jnp.float32)
    for a in (-1, 0, 1):
        for b in (-1, 0, 1):
            for c in (-1, 0, 1):
                d = 9 * (a + 1) + 3 * (b + 1) + (c + 1)
                range_a = source_range(a)
                range_b = source_range(b)
                range_c = source_range(c)
                result = result.at[tile_table[:, d], range_a[0], range_b[0], range_c[0]].add(
                    padded[:, range_a[1], range_b[1], range_c[1]]
                )
    return result


def section_x(values, steps):
    return shifted(values, "gx", steps)


def section_y(values, steps):
    return shifted(values, "gy", steps)


def return_x(values, steps):
    return shifted(values.astype(jnp.bfloat16), "gx", steps).astype(values.dtype)


def return_y(values, steps):
    return shifted(values.astype(jnp.bfloat16), "gy", steps).astype(values.dtype)


def extend(field, face_list, corner_list):
    side = face_list.shape[1]
    small = corner_list.shape[1]
    faces = [jnp.take(field, face_list[k], axis=0) for k in range(4)]
    corners = [jnp.take(field, corner_list[k], axis=0) for k in range(4)]
    upper_x = section_x(jnp.concatenate([faces[0], corners[0], corners[1]], axis=0), 1)
    lower_x = section_x(jnp.concatenate([faces[1], corners[2], corners[3]], axis=0), -1)
    upper_y = section_y(
        jnp.concatenate(
            [faces[2], upper_x[side : side + small], lower_x[side : side + small]], axis=0
        ),
        1,
    )
    lower_y = section_y(
        jnp.concatenate([faces[3], upper_x[side + small :], lower_x[side + small :]], axis=0), -1
    )
    got_faces = [upper_x[:side], lower_x[:side], upper_y[:side], lower_y[:side]]
    got_corners = [
        upper_y[side : side + small],
        lower_y[side : side + small],
        upper_y[side + small :],
        lower_y[side + small :],
    ]
    zero_brick = jnp.zeros((1,) + field.shape[1:], field.dtype)
    return jnp.concatenate([field] + got_faces + got_corners + [zero_brick], axis=0)


def return_home(ext_grads, face_list, corner_list, bricks):
    side = face_list.shape[1]
    small = corner_list.shape[1]
    start = bricks + 4 * side
    grad_faces = [ext_grads[bricks + k * side : bricks + (k + 1) * side] for k in range(4)]
    grad_corners = [ext_grads[start + k * small : start + (k + 1) * small] for k in range(4)]
    lower_y = return_y(
        jnp.concatenate([grad_faces[2], grad_corners[0], grad_corners[2]], axis=0), -1
    )
    upper_y = return_y(
        jnp.concatenate([grad_faces[3], grad_corners[1], grad_corners[3]], axis=0), 1
    )
    lower_x = return_x(
        jnp.concatenate(
            [grad_faces[0], lower_y[side : side + small], upper_y[side : side + small]], axis=0
        ),
        -1,
    )
    upper_x = return_x(
        jnp.concatenate([grad_faces[1], lower_y[side + small :], upper_y[side + small :]], axis=0),
        1,
    )
    home_faces = [lower_x[:side], upper_x[:side], lower_y[:side], upper_y[:side]]
    home_corners = [
        lower_x[side : side + small],
        lower_x[side + small :],
        upper_x[side : side + small],
        upper_x[side + small :],
    ]
    result = ext_grads[:bricks]
    for k in range(4):
        result = result.at[face_list[k]].add(home_faces[k])
        result = result.at[corner_list[k]].add(home_corners[k])
    return result


def moments(values, occupied, weighted):
    return lax.psum(
        (weighted, jnp.sum(values * occupied, axis=0), jnp.sum(values * values * occupied, axis=0)),
        ("gx", "gy"),
    )


def normalize(values, totals):
    center = totals[1] / totals[0]
    spread_sq = totals[2] / totals[0] - center * center
    recip = lax.rsqrt(spread_sq + epsilon)
    return ((values - center) * recip, recip)


def conv_back(columns, grads, flat, kernel_map, face_list, corner_list, bricks, channels, total):
    partial_w = lax.dot_general(
        columns, grads, (((0,), (0,)), ((), ())), preferred_element_type=jnp.float32
    )
    spread_cols = lax.dot_general(
        grads, flat, (((1,), (1,)), ((), ())), preferred_element_type=jnp.float32
    )
    ext_grads = scatter_bricks(spread(spread_cols, bricks, channels), kernel_map, total)
    homed = return_home(ext_grads, face_list, corner_list, bricks)
    return (partial_w, homed.reshape(bricks * 64, channels))


def body(
    voxel_feats,
    w_first,
    w_second,
    norm_gain,
    norm_shift,
    grad_out,
    brick_count,
    kernel_map,
    face_send,
    corner_send,
):
    bricks = voxel_feats.shape[0]
    channels = voxel_feats.shape[2]
    face_list = face_send[0]
    corner_list = corner_send[0]
    total = bricks + 4 * face_list.shape[1] + 4 * corner_list.shape[1] + 1
    shape_five = (bricks, 4, 4, 4, channels)
    occupied = (lax.broadcasted_iota(jnp.int32, (bricks * 64, 1), 0) // 64 < brick_count[0]).astype(
        jnp.float32
    )
    feats = voxel_feats.reshape(bricks * 64, channels) * occupied.astype(jnp.bfloat16)
    flat_one = w_first.reshape(27 * channels, channels)
    flat_two = w_second.reshape(27 * channels, channels)
    cols_one = patches(
        assemble(extend(feats.reshape(shape_five), face_list, corner_list), kernel_map)
    )
    z_one = jnp.dot(cols_one, flat_one, preferred_element_type=jnp.float32)
    weighted = 64.0 * brick_count[0].astype(jnp.float32)
    totals_one = moments(z_one, occupied, weighted)
    voxels = totals_one[0]
    xh_one, recip_one = normalize(z_one, totals_one)
    u_one = norm_gain[0] * xh_one + norm_shift[0]
    a_one = (jax.nn.silu(u_one) * occupied).astype(jnp.bfloat16)
    cols_two = patches(
        assemble(extend(a_one.reshape(shape_five), face_list, corner_list), kernel_map)
    )
    z_two = jnp.dot(cols_two, flat_two, preferred_element_type=jnp.float32)
    xh_two, recip_two = normalize(z_two, moments(z_two, occupied, weighted))
    pre = norm_gain[1] * xh_two + norm_shift[1] + feats.astype(jnp.float32)
    out_feats = (jax.nn.silu(pre) * occupied).astype(jnp.bfloat16)
    d_val = grad_out.reshape(bricks * 64, channels).astype(jnp.float32) * occupied * silu_slope(pre)
    sum_two, cross_two = lax.psum(
        (jnp.sum(d_val, axis=0), jnp.sum(d_val * xh_two, axis=0)), ("gx", "gy")
    )
    dz_two = (
        occupied
        * norm_gain[1]
        * recip_two
        * (d_val - sum_two / voxels - xh_two * cross_two / voxels)
    ).astype(jnp.bfloat16)
    dw_two, da_one = conv_back(
        cols_two, dz_two, flat_two, kernel_map, face_list, corner_list, bricks, channels, total
    )
    du_one = da_one * occupied * silu_slope(u_one)
    sum_one, cross_one = lax.psum(
        (jnp.sum(du_one, axis=0), jnp.sum(du_one * xh_one, axis=0)), ("gx", "gy")
    )
    dz_one = (
        occupied
        * norm_gain[0]
        * recip_one
        * (du_one - sum_one / voxels - xh_one * cross_one / voxels)
    ).astype(jnp.bfloat16)
    dw_one, back_in = conv_back(
        cols_one, dz_one, flat_one, kernel_map, face_list, corner_list, bricks, channels, total
    )
    grad_in = ((d_val + back_in) * occupied).astype(jnp.bfloat16)
    dw_one, dw_two = lax.psum((dw_one, dw_two), ("gx", "gy"))
    root = jnp.sqrt(voxels)
    weight_grads = jnp.stack([dw_one, dw_two]).reshape(2, 27, channels, channels) / root
    norm_grads = jnp.stack([cross_one, sum_one, cross_two, sum_two]) / root
    return (
        out_feats.reshape(bricks, 64, channels),
        grad_in.reshape(bricks, 64, channels),
        weight_grads,
        norm_grads,
    )


def solution(mesh):
    in_specs = (
        P(("gx", "gy"), None, None),
        P(),
        P(),
        P(),
        P(),
        P(("gx", "gy"), None, None),
        P(("gx", "gy")),
        P(("gx", "gy"), None),
        P(("gx", "gy"), None, None),
        P(("gx", "gy"), None, None),
    )
    out_specs = (P(("gx", "gy"), None, None), P(("gx", "gy"), None, None), P(), P())
    return jax.shard_map(body, mesh=mesh, in_specs=in_specs, out_specs=out_specs, check_vma=False)
```

profile of v0, /device:TPU:0, one launch (start us, length us, event | category | flops | bytes accessed | tf_op | source)
XLA Modules:
  0.0 2442.6 jit_solution(14212458251181931822)
XLA Ops:
  28.8 5.5 collective-permute-start
  120.6 42.8 %all-reduce.17 = (f32[128]{0:T(128)S(1)}, f32[]{:T(128)}, f32[128]{0:T(128)S(1)}) all-reduce(f32[128]{0:T(128)S(1)} %get-tuple-element.1427, f32[]{:T(128)S(6)} %mul_shard_map.3, f32[128]{0:T(128)S(1)} %get-tuple-element.1426), channel_id=1, replica_groups=mesh['gx'=4,'gy'=8] {'gx','gy'}, use_global_device_ids=true, to_apply=%region_1.11 | all-reduce | flops 257 | bytes 2056 | tf_op jit(solution)/shard_map/psum | solution.py:159
  166.9 4.8 collective-permute-start.4
  262.3 44.3 %all-reduce.16 = (f32[128]{0:T(128)S(1)}, f32[128]{0:T(128)S(1)}) all-reduce(f32[128]{0:T(128)S(1)} %get-tuple-element.1425, f32[128]{0:T(128)S(1)} %get-tuple-element.1424), channel_id=1, replica_groups=mesh['gx'=4,'gy'=8] {'gx','gy'}, use_global_device_ids=true, to_apply=%region_6.16 | all-reduce | flops 256 | bytes 2048 | tf_op jit(solution)/shard_map/psum | solution.py:159
  308.1 40.3 %all-reduce.15 = (f32[128]{0:T(128)S(1)}, f32[128]{0:T(128)S(1)}) all-reduce(f32[128]{0:T(128)S(1)} %get-tuple-element.1431, f32[128]{0:T(128)S(1)} %get-tuple-element.1430), channel_id=1, replica_groups=mesh['gx'=4,'gy'=8] {'gx','gy'}, use_global_device_ids=true, to_apply=%region_12.22 | all-reduce | flops 256 | bytes 2048 | tf_op jit(solution)/shard_map/psum | solution.py:226
  419.0 4.2 fusion.155
  423.3 41.3 %while.123 = (s32[]{:T(128)}, f32[13,4,4,4,128]{4,3,2,1,0:T(4,128)S(1)}, s32[4,4]{1,0:T(4,128)S(1)}, f32[4,1,1,1,128]{4,3,2,1,0:T(1,128)}, s32[]{:T(128)}, /*index=5*/s32[5]{0:T(128)S(1)}, s32[1]{0:T(128)}, s32[]{:T(128)}) while((s32[]{:T(128)}, f32[13,4,4,4,128]{4,3,2,1,0:T(4,128)S(1)}, s32[4,4]{1,0:T(4,128)S(1)}, ...), condition=%wide.while_cond.71, body=%wide.while_body.71.sunk | while | flops 277 | bytes 2819 | solution.py:73
  464.6 26.0 %while.124 = (s32[]{:T(128)}, f32[13,4,4,4,128]{4,3,2,1,0:T(4,128)S(1)}, s32[4,3]{1,0:T(4,128)S(1)}, f32[4,1,1,4,128]{4,3,2,1,0:T(4,128)}, s32[]{:T(128)}, /*index=5*/s32[5]{0:T(128)S(1)}, s32[1]{0:T(128)}) while((s32[]{:T(128)}, f32[13,4,4,4,128]{4,3,2,1,0:T(4,128)S(1)}, s32[4,3]{1,0:T(4,128)S(1)}, f32[4,1,1,4,128]{4,3,2,1,0:T(4,128)}, ...), condition=%wide.while_cond.72, body=%wide.while_body.72.sunk | while | flops 1045 | bytes 6371 | solution.py:73
  490.6 41.3 %while.125 = (s32[]{:T(128)}, f32[13,4,4,4,128]{4,3,2,1,0:T(4,128)S(1)}, s32[4,4]{1,0:T(4,128)S(1)}, f32[4,1,1,1,128]{4,3,2,1,0:T(1,128)}, s32[]{:T(128)}, /*index=5*/s32[5]{0:T(128)S(1)}, s32[1]{0:T(128)}, s32[]{:T(128)}) while((s32[]{:T(128)}, f32[13,4,4,4,128]{4,3,2,1,0:T(4,128)S(1)}, s32[4,4]{1,0:T(4,128)S(1)}, ...), condition=%wide.while_cond.73, body=%wide.while_body.73.sunk | while | flops 277 | bytes 2819 | solution.py:73
  532.5 33.7 %while.126 = (s32[]{:T(128)}, f32[13,4,4,4,128]{4,3,2,1,0:T(4,128)S(1)}, s32[4,3]{1,0:T(4,128)S(1)}, f32[4,1,4,1,128]{4,3,2,1,0:T(1,128)}, s32[]{:T(128)}, /*index=5*/s32[5]{0:T(128)S(1)}, s32[1]{0:T(128)}, s32[]{:T(128)}) while((s32[]{:T(128)}, f32[13,4,4,4,128]{4,3,2,1,0:T(4,128)S(1)}, s32[4,3]{1,0:T(4,128)S(1)}, ...), condition=%wide.while_cond.74, body=%wide.while_body.74.sunk | while | flops 1045 | bytes 10479 | solution.py:73
  566.2 23.6 while.127
  589.8 39.2 %while.128 = (s32[]{:T(128)}, f32[13,4,4,4,128]{4,3,2,1,0:T(4,128)S(1)}, s32[4,3]{1,0:T(4,128)}, f32[4,1,4,1,128]{4,3,2,1,0:T(1,128)}, s32[]{:T(128)}, /*index=5*/s32[5]{0:T(128)}, s32[1]{0:T(128)}, s32[]{:T(128)}) while((s32[]{:T(128)}, f32[13,4,4,4,128]{4,3,2,1,0:T(4,128)S(1)}, s32[4,3]{1,0:T(4,128)}, f32[4,1,4,1,128]{4,3,2,1,0:T(1,128)}, ...), condition=%wide.while_cond.76, body=%wide.while_body.76.sunk | while | flops 1045 | bytes 10479 | solution.py:73
  629.0 46.6 %while.129 = (s32[]{:T(128)}, f32[13,4,4,4,128]{4,3,2,1,0:T(4,128)S(1)}, s32[4,4]{1,0:T(4,128)}, f32[4,1,1,1,128]{4,3,2,1,0:T(1,128)}, s32[]{:T(128)}, /*index=5*/s32[5]{0:T(128)}, s32[1]{0:T(128)}, s32[]{:T(128)}) while((s32[]{:T(128)}, f32[13,4,4,4,128]{4,3,2,1,0:T(4,128)S(1)}, s32[4,4]{1,0:T(4,128)}, f32[4,1,1,1,128]{4,3,2,1,0:T(1,128)}, ...), condition=%wide.while_cond.77, body=%wide.while_body.77.sunk | while | flops 277 | bytes 2819 | solution.py:73
  675.6 31.5 %while.130 = (s32[]{:T(128)}, f32[13,4,4,4,128]{4,3,2,1,0:T(4,128)S(1)}, s32[4,3]{1,0:T(4,128)}, f32[4,1,1,4,128]{4,3,2,1,0:T(4,128)}, s32[]{:T(128)}, /*index=5*/s32[5]{0:T(128)}, s32[1]{0:T(128)}) while((s32[]{:T(128)}, f32[13,4,4,4,128]{4,3,2,1,0:T(4,128)S(1)}, s32[4,3]{1,0:T(4,128)}, f32[4,1,1,4,128]{4,3,2,1,0:T(4,128)}, s32[]{:T(128)}, ...), condition=%wide.while_cond.78, body=%wide.while_body.78.sunk | while | flops 1045 | bytes 6371 | solution.py:73
  707.1 44.0 %while.131 = (s32[]{:T(128)}, f32[13,4,4,4,128]{4,3,2,1,0:T(4,128)S(1)}, s32[4,4]{1,0:T(4,128)S(1)}, f32[4,1,1,1,128]{4,3,2,1,0:T(1,128)}, s32[]{:T(128)}, /*index=5*/s32[5]{0:T(128)}, s32[1]{0:T(128)}, s32[]{:T(128)}) while((s32[]{:T(128)}, f32[13,4,4,4,128]{4,3,2,1,0:T(4,128)S(1)}, s32[4,4]{1,0:T(4,128)S(1)}, f32[4,1,1,1,128]{4,3,2,1,0:T(1,128)}, ...), condition=%wide.while_cond.79, body=%wide.while_body.79.sunk | while | flops 277 | bytes 2819 | solution.py:73
  751.1 36.5 %while.132 = (s32[]{:T(128)}, f32[13,4,4,4,128]{4,3,2,1,0:T(4,128)S(1)}, s32[4,3]{1,0:T(4,128)S(1)}, f32[4,4,1,1,128]{4,3,2,1,0:T(1,128)}, s32[]{:T(128)}, /*index=5*/s32[5]{0:T(128)}, s32[1]{0:T(128)}, s32[]{:T(128)}) while((s32[]{:T(128)}, f32[13,4,4,4,128]{4,3,2,1,0:T(4,128)S(1)}, s32[4,3]{1,0:T(4,128)S(1)}, f32[4,4,1,1,128]{4,3,2,1,0:T(1,128)}, ...), condition=%wide.while_cond.80, body=%wide.while_body.80.sunk | while | flops 1045 | bytes 10479 | solution.py:73
  787.6 23.9 while.133
  811.5 37.9 %while.134 = (s32[]{:T(128)}, f32[13,4,4,4,128]{4,3,2,1,0:T(4,128)S(1)}, s32[4,3]{1,0:T(4,128)}, f32[4,4,1,1,128]{4,3,2,1,0:T(1,128)}, s32[]{:T(128)}, /*index=5*/s32[5]{0:T(128)}, s32[1]{0:T(128)}, s32[]{:T(128)}) while((s32[]{:T(128)}, f32[13,4,4,4,128]{4,3,2,1,0:T(4,128)S(1)}, s32[4,3]{1,0:T(4,128)}, f32[4,4,1,1,128]{4,3,2,1,0:T(1,128)}, ...), condition=%wide.while_cond.82, body=%wide.while_body.82.sunk | while | flops 1045 | bytes 10479 | solution.py:73
  849.4 28.8 %while.135 = (s32[]{:T(128)}, f32[13,4,4,4,128]{4,3,2,1,0:T(4,128)S(1)}, s32[4,2]{0,1:T(2,128)S(1)}, f32[4,4,4,1,128]{4,3,2,1,0:T(1,128)}, s32[]{:T(128)}, /*index=5*/s32[5]{0:T(128)}, s32[1]{0:T(128)}, s32[]{:T(128)}) while((s32[]{:T(128)}, f32[13,4,4,4,128]{4,3,2,1,0:T(4,128)S(1)}, s32[4,2]{0,1:T(2,128)S(1)}, f32[4,4,4,1,128]{4,3,2,1,0:T(1,128)}, ...), condition=%wide.while_cond.83, body=%wide.while_body.83.sunk | while | flops 4117 | bytes 41179 | solution.py:73
  879.0 29.4 %while.136 = (s32[]{:T(128)}, f32[13,4,4,4,128]{4,3,2,1,0:T(4,128)S(1)}, s32[4,2]{0,1:T(2,128)S(1)}, f32[4,4,4,1,128]{4,3,2,1,0:T(1,128)}, s32[]{:T(128)}, /*index=5*/s32[5]{0:T(128)}, s32[1]{0:T(128)}, s32[]{:T(128)}) while((s32[]{:T(128)}, f32[13,4,4,4,128]{4,3,2,1,0:T(4,128)S(1)}, s32[4,2]{0,1:T(2,128)S(1)}, f32[4,4,4,1,128]{4,3,2,1,0:T(1,128)}, ...), condition=%wide.while_cond.84, body=%wide.while_body.84.sunk | while | flops 4117 | bytes 41179 | solution.py:73
  908.4 36.8 %while.137 = (s32[]{:T(128)}, f32[13,4,4,4,128]{4,3,2,1,0:T(4,128)S(1)}, s32[4,3]{1,0:T(4,128)S(1)}, f32[4,4,1,1,128]{4,3,2,1,0:T(1,128)}, s32[]{:T(128)}, /*index=5*/s32[5]{0:T(128)}, s32[1]{0:T(128)}, s32[]{:T(128)}) while((s32[]{:T(128)}, f32[13,4,4,4,128]{4,3,2,1,0:T(4,128)S(1)}, s32[4,3]{1,0:T(4,128)S(1)}, f32[4,4,1,1,128]{4,3,2,1,0:T(1,128)}, ...), condition=%wide.while_cond.85, body=%wide.while_body.85.sunk | while | flops 1045 | bytes 10479 | solution.py:73
  945.2 23.9 while.138
  969.1 39.5 %while.139 = (s32[]{:T(128)}, f32[13,4,4,4,128]{4,3,2,1,0:T(4,128)S(1)}, s32[4,3]{1,0:T(4,128)}, f32[4,4,1,1,128]{4,3,2,1,0:T(1,128)}, s32[]{:T(128)}, /*index=5*/s32[5]{0:T(128)}, s32[1]{0:T(128)}, s32[]{:T(128)}) while((s32[]{:T(128)}, f32[13,4,4,4,128]{4,3,2,1,0:T(4,128)S(1)}, s32[4,3]{1,0:T(4,128)}, f32[4,4,1,1,128]{4,3,2,1,0:T(1,128)}, ...), condition=%wide.while_cond.87, body=%wide.while_body.87.sunk | while | flops 1045 | bytes 10479 | solution.py:73
  1008.6 47.0 %while.140 = (s32[]{:T(128)}, f32[13,4,4,4,128]{4,3,2,1,0:T(4,128)S(1)}, s32[4,4]{1,0:T(4,128)}, f32[4,1,1,1,128]{4,3,2,1,0:T(1,128)}, s32[]{:T(128)}, /*index=5*/s32[5]{0:T(128)}, s32[1]{0:T(128)}, s32[]{:T(128)}) while((s32[]{:T(128)}, f32[13,4,4,4,128]{4,3,2,1,0:T(4,128)S(1)}, s32[4,4]{1,0:T(4,128)}, f32[4,1,1,1,128]{4,3,2,1,0:T(1,128)}, ...), condition=%wide.while_cond.88, body=%wide.while_body.88.sunk | while | flops 277 | bytes 2819 | solution.py:73
  1055.6 31.7 %while.141 = (s32[]{:T(128)}, f32[13,4,4,4,128]{4,3,2,1,0:T(4,128)S(1)}, s32[4,3]{1,0:T(4,128)}, f32[4,1,1,4,128]{4,3,2,1,0:T(4,128)}, s32[]{:T(128)}, /*index=5*/s32[5]{0:T(128)}, s32[1]{0:T(128)}) while((s32[]{:T(128)}, f32[13,4,4,4,128]{4,3,2,1,0:T(4,128)S(1)}, s32[4,3]{1,0:T(4,128)}, f32[4,1,1,4,128]{4,3,2,1,0:T(4,128)}, s32[]{:T(128)}, ...), condition=%wide.while_cond.89, body=%wide.while_body.89.sunk | while | flops 1045 | bytes 6371 | solution.py:73
  1087.2 47.0 %while.142 = (s32[]{:T(128)}, f32[13,4,4,4,128]{4,3,2,1,0:T(4,128)S(1)}, s32[4,4]{1,0:T(4,128)}, f32[4,1,1,1,128]{4,3,2,1,0:T(1,128)}, s32[]{:T(128)}, /*index=5*/s32[5]{0:T(128)}, s32[1]{0:T(128)}, s32[]{:T(128)}) while((s32[]{:T(128)}, f32[13,4,4,4,128]{4,3,2,1,0:T(4,128)S(1)}, s32[4,4]{1,0:T(4,128)}, f32[4,1,1,1,128]{4,3,2,1,0:T(1,128)}, ...), condition=%wide.while_cond.90, body=%wide.while_body.90.sunk | while | flops 277 | bytes 2819 | solution.py:73
  1092.6 3.9 broadcast_select_fusion.131
  1134.2 39.2 %while.143 = (s32[]{:T(128)}, f32[13,4,4,4,128]{4,3,2,1,0:T(4,128)S(1)}, s32[4,3]{1,0:T(4,128)}, f32[4,1,4,1,128]{4,3,2,1,0:T(1,128)}, s32[]{:T(128)}, /*index=5*/s32[5]{0:T(128)}, s32[1]{0:T(128)}, s32[]{:T(128)}) while((s32[]{:T(128)}, f32[13,4,4,4,128]{4,3,2,1,0:T(4,128)S(1)}, s32[4,3]{1,0:T(4,128)}, f32[4,1,4,1,128]{4,3,2,1,0:T(1,128)}, ...), condition=%wide.while_cond.91, body=%wide.while_body.91.sunk | while | flops 1045 | bytes 10479 | solution.py:73
  1173.5 21.2 while.144
  1194.7 36.8 %while.145 = (s32[]{:T(128)}, f32[13,4,4,4,128]{4,3,2,1,0:T(4,128)S(1)}, s32[4,3]{1,0:T(4,128)S(1)}, f32[4,1,4,1,128]{4,3,2,1,0:T(1,128)}, s32[]{:T(128)}, /*index=5*/s32[5]{0:T(128)}, s32[1]{0:T(128)}, s32[]{:T(128)}) while((s32[]{:T(128)}, f32[13,4,4,4,128]{4,3,2,1,0:T(4,128)S(1)}, s32[4,3]{1,0:T(4,128)S(1)}, f32[4,1,4,1,128]{4,3,2,1,0:T(1,128)}, ...), condition=%wide.while_cond.93, body=%wide.while_body.93.sunk | while | flops 1045 | bytes 10479 | solution.py:73
  1231.5 55.2 %while.146 = (s32[]{:T(128)}, f32[13,4,4,4,128]{4,3,2,1,0:T(4,128)S(1)}, s32[4,4]{1,0:T(4,128)S(1)}, f32[4,1,1,1,128]{4,3,2,1,0:T(1,128)}, s32[]{:T(128)}, /*index=5*/s32[5]{0:T(128)}, s32[1]{0:T(128)}, s32[]{:T(128)}) while((s32[]{:T(128)}, f32[13,4,4,4,128]{4,3,2,1,0:T(4,128)S(1)}, s32[4,4]{1,0:T(4,128)S(1)}, f32[4,1,1,1,128]{4,3,2,1,0:T(1,128)}, ...), condition=%wide.while_cond.94, body=%wide.while_body.94.sunk | while | flops 277 | bytes 2819 | solution.py:73
  1286.7 26.4 %while.147 = (s32[]{:T(128)}, f32[13,4,4,4,128]{4,3,2,1,0:T(4,128)S(1)}, s32[4,3]{1,0:T(4,128)S(1)}, f32[4,1,1,4,128]{4,3,2,1,0:T(4,128)}, s32[]{:T(128)}, /*index=5*/s32[5]{0:T(128)S(1)}, s32[1]{0:T(128)}) while((s32[]{:T(128)}, f32[13,4,4,4,128]{4,3,2,1,0:T(4,128)S(1)}, s32[4,3]{1,0:T(4,128)S(1)}, f32[4,1,1,4,128]{4,3,2,1,0:T(4,128)}, ...), condition=%wide.while_cond.95, body=%wide.while_body.95.sunk | while | flops 1045 | bytes 6371 | solution.py:73
  1313.1 41.7 %while.148 = (s32[]{:T(128)}, f32[13,4,4,4,128]{4,3,2,1,0:T(4,128)S(1)}, s32[4,4]{1,0:T(4,128)S(1)}, f32[4,1,1,1,128]{4,3,2,1,0:T(1,128)S(1)}, s32[]{:T(128)}, /*index=5*/s32[5]{0:T(128)}, s32[1]{0:T(128)}, s32[]{:T(128)}) while((s32[]{:T(128)}, f32[13,4,4,4,128]{4,3,2,1,0:T(4,128)S(1)}, s32[4,4]{1,0:T(4,128)S(1)}, ...), condition=%wide.while_cond.96, body=%wide.while_body.96.sunk | while | flops 277 | bytes 2819 | solution.py:73
  1361.7 4.8 collective-permute-start.11
  1372.8 44.2 %all-reduce.14 = (f32[128]{0:T(128)S(1)}, f32[128]{0:T(128)S(1)}) all-reduce(f32[128]{0:T(128)S(1)} %get-tuple-element.1429, f32[128]{0:T(128)S(1)} %get-tuple-element.1428), channel_id=1, replica_groups=mesh['gx'=4,'gy'=8] {'gx','gy'}, use_global_device_ids=true, to_apply=%region_51.61 | all-reduce | flops 256 | bytes 2048 | tf_op jit(solution)/shard_map/psum | solution.py:239
  1459.2 41.1 %while.149 = (s32[]{:T(128)}, f32[13,4,4,4,128]{4,3,2,1,0:T(4,128)S(1)}, s32[4,4]{1,0:T(4,128)}, f32[4,1,1,1,128]{4,3,2,1,0:T(1,128)S(1)}, s32[]{:T(128)}, /*index=5*/s32[5]{0:T(128)S(1)}, s32[1]{0:T(128)}, s32[]{:T(128)}) while((s32[]{:T(128)}, f32[13,4,4,4,128]{4,3,2,1,0:T(4,128)S(1)}, s32[4,4]{1,0:T(4,128)}, ...), condition=%wide.while_cond.97, body=%wide.while_body.97.sunk | while | flops 277 | bytes 2819 | solution.py:73
  1500.3 25.5 %while.150 = (s32[]{:T(128)}, f32[13,4,4,4,128]{4,3,2,1,0:T(4,128)S(1)}, s32[4,3]{1,0:T(4,128)}, f32[4,1,1,4,128]{4,3,2,1,0:T(4,128)S(1)}, s32[]{:T(128)}, /*index=5*/s32[5]{0:T(128)S(1)}, s32[1]{0:T(128)}) while((s32[]{:T(128)}, f32[13,4,4,4,128]{4,3,2,1,0:T(4,128)S(1)}, s32[4,3]{1,0:T(4,128)}, f32[4,1,1,4,128]{4,3,2,1,0:T(4,128)S(1)}, ...), condition=%wide.while_cond.98, body=%wide.while_body.98.sunk | while | flops 1045 | bytes 6371 | solution.py:73
  1525.8 40.4 %while.151 = (s32[]{:T(128)}, f32[13,4,4,4,128]{4,3,2,1,0:T(4,128)S(1)}, s32[4,4]{1,0:T(4,128)}, f32[4,1,1,1,128]{4,3,2,1,0:T(1,128)S(1)}, s32[]{:T(128)}, /*index=5*/s32[5]{0:T(128)S(1)}, s32[1]{0:T(128)}, s32[]{:T(128)}) while((s32[]{:T(128)}, f32[13,4,4,4,128]{4,3,2,1,0:T(4,128)S(1)}, s32[4,4]{1,0:T(4,128)}, ...), condition=%wide.while_cond.99, body=%wide.while_body.99.sunk | while | flops 277 | bytes 2819 | solution.py:73
  1566.2 33.8 %while.152 = (s32[]{:T(128)}, f32[13,4,4,4,128]{4,3,2,1,0:T(4,128)S(1)}, s32[4,3]{1,0:T(4,128)}, f32[4,1,4,1,128]{4,3,2,1,0:T(1,128)S(1)}, s32[]{:T(128)}, /*index=5*/s32[5]{0:T(128)S(1)}, s32[1]{0:T(128)}, s32[]{:T(128)}) while((s32[]{:T(128)}, f32[13,4,4,4,128]{4,3,2,1,0:T(4,128)S(1)}, s32[4,3]{1,0:T(4,128)}, ...), condition=%wide.while_cond.100, body=%wide.while_body.100.sunk | while | flops 1045 | bytes 10479 | solution.py:73
  1600.0 18.7 while.153
  1618.7 34.2 %while.154 = (s32[]{:T(128)}, f32[13,4,4,4,128]{4,3,2,1,0:T(4,128)S(1)}, s32[4,3]{1,0:T(4,128)}, f32[4,1,4,1,128]{4,3,2,1,0:T(1,128)S(1)}, s32[]{:T(128)}, /*index=5*/s32[5]{0:T(128)S(1)}, s32[1]{0:T(128)}, s32[]{:T(128)}) while((s32[]{:T(128)}, f32[13,4,4,4,128]{4,3,2,1,0:T(4,128)S(1)}, s32[4,3]{1,0:T(4,128)}, ...), condition=%wide.while_cond.102, body=%wide.while_body.102.sunk | while | flops 1045 | bytes 10479 | solution.py:73
  1653.0 42.2 %while.155 = (s32[]{:T(128)}, f32[13,4,4,4,128]{4,3,2,1,0:T(4,128)S(1)}, s32[4,4]{1,0:T(4,128)}, f32[4,1,1,1,128]{4,3,2,1,0:T(1,128)S(1)}, s32[]{:T(128)}, /*index=5*/s32[5]{0:T(128)S(1)}, s32[1]{0:T(128)}, s32[]{:T(128)}) while((s32[]{:T(128)}, f32[13,4,4,4,128]{4,3,2,1,0:T(4,128)S(1)}, s32[4,4]{1,0:T(4,128)}, ...), condition=%wide.while_cond.103, body=%wide.while_body.103.sunk | while | flops 277 | bytes 2819 | solution.py:73
  1695.2 26.6 %while.156 = (s32[]{:T(128)}, f32[13,4,4,4,128]{4,3,2,1,0:T(4,128)S(1)}, s32[4,3]{1,0:T(4,128)}, f32[4,1,1,4,128]{4,3,2,1,0:T(4,128)S(1)}, s32[]{:T(128)}, /*index=5*/s32[5]{0:T(128)S(1)}, s32[1]{0:T(128)}) while((s32[]{:T(128)}, f32[13,4,4,4,128]{4,3,2,1,0:T(4,128)S(1)}, s32[4,3]{1,0:T(4,128)}, f32[4,1,1,4,128]{4,3,2,1,0:T(4,128)S(1)}, ...), condition=%wide.while_cond.104, body=%wide.while_body.104.sunk | while | flops 1045 | bytes 6371 | solution.py:73
  1721.8 42.1 %while.157 = (s32[]{:T(128)}, f32[13,4,4,4,128]{4,3,2,1,0:T(4,128)S(1)}, s32[4,4]{1,0:T(4,128)}, f32[4,1,1,1,128]{4,3,2,1,0:T(1,128)S(1)}, s32[]{:T(128)}, /*index=5*/s32[5]{0:T(128)S(1)}, s32[1]{0:T(128)}, s32[]{:T(128)}) while((s32[]{:T(128)}, f32[13,4,4,4,128]{4,3,2,1,0:T(4,128)S(1)}, s32[4,4]{1,0:T(4,128)}, ...), condition=%wide.while_cond.105, body=%wide.while_body.105.sunk | while | flops 277 | bytes 2819 | solution.py:73
  1763.9 34.0 %while.158 = (s32[]{:T(128)}, f32[13,4,4,4,128]{4,3,2,1,0:T(4,128)S(1)}, s32[4,3]{1,0:T(4,128)}, f32[4,4,1,1,128]{4,3,2,1,0:T(1,128)S(1)}, s32[]{:T(128)}, /*index=5*/s32[5]{0:T(128)S(1)}, s32[1]{0:T(128)}, s32[]{:T(128)}) while((s32[]{:T(128)}, f32[13,4,4,4,128]{4,3,2,1,0:T(4,128)S(1)}, s32[4,3]{1,0:T(4,128)}, ...), condition=%wide.while_cond.106, body=%wide.while_body.106.sunk | while | flops 1045 | bytes 10479 | solution.py:73
  1797.9 18.2 while.159
  1816.1 33.9 %while.160 = (s32[]{:T(128)}, f32[13,4,4,4,128]{4,3,2,1,0:T(4,128)S(1)}, s32[4,3]{1,0:T(4,128)}, f32[4,4,1,1,128]{4,3,2,1,0:T(1,128)S(1)}, s32[]{:T(128)}, /*index=5*/s32[5]{0:T(128)S(1)}, s32[1]{0:T(128)}, s32[]{:T(128)}) while((s32[]{:T(128)}, f32[13,4,4,4,128]{4,3,2,1,0:T(4,128)S(1)}, s32[4,3]{1,0:T(4,128)}, ...), condition=%wide.while_cond.108, body=%wide.while_body.108.sunk | while | flops 1045 | bytes 10479 | solution.py:73
  1850.0 24.3 while.161
  1875.1 24.4 while.162
  1899.5 34.4 %while.163 = (s32[]{:T(128)}, f32[13,4,4,4,128]{4,3,2,1,0:T(4,128)S(1)}, s32[4,3]{1,0:T(4,128)}, f32[4,4,1,1,128]{4,3,2,1,0:T(1,128)S(1)}, s32[]{:T(128)}, /*index=5*/s32[5]{0:T(128)S(1)}, s32[1]{0:T(128)}, s32[]{:T(128)}) while((s32[]{:T(128)}, f32[13,4,4,4,128]{4,3,2,1,0:T(4,128)S(1)}, s32[4,3]{1,0:T(4,128)}, ...), condition=%wide.while_cond.111, body=%wide.while_body.111.sunk | while | flops 1045 | bytes 10479 | solution.py:73
  1933.9 18.1 while.164
  1952.0 33.6 %while.165 = (s32[]{:T(128)}, f32[13,4,4,4,128]{4,3,2,1,0:T(4,128)S(1)}, s32[4,3]{1,0:T(4,128)}, f32[4,4,1,1,128]{4,3,2,1,0:T(1,128)S(1)}, s32[]{:T(128)}, /*index=5*/s32[5]{0:T(128)S(1)}, s32[1]{0:T(128)}, s32[]{:T(128)}) while((s32[]{:T(128)}, f32[13,4,4,4,128]{4,3,2,1,0:T(4,128)S(1)}, s32[4,3]{1,0:T(4,128)}, ...), condition=%wide.while_cond.113, body=%wide.while_body.113.sunk | while | flops 1045 | bytes 10479 | solution.py:73
  1985.6 40.4 %while.166 = (s32[]{:T(128)}, f32[13,4,4,4,128]{4,3,2,1,0:T(4,128)S(1)}, s32[4,4]{1,0:T(4,128)}, f32[4,1,1,1,128]{4,3,2,1,0:T(1,128)S(1)}, s32[]{:T(128)}, /*index=5*/s32[5]{0:T(128)S(1)}, s32[1]{0:T(128)}, s32[]{:T(128)}) while((s32[]{:T(128)}, f32[13,4,4,4,128]{4,3,2,1,0:T(4,128)S(1)}, s32[4,4]{1,0:T(4,128)}, ...), condition=%wide.while_cond.114, body=%wide.while_body.114.sunk | while | flops 277 | bytes 2819 | solution.py:73
  2026.0 25.5 %while.167 = (s32[]{:T(128)}, f32[13,4,4,4,128]{4,3,2,1,0:T(4,128)S(1)}, s32[4,3]{1,0:T(4,128)}, f32[4,1,1,4,128]{4,3,2,1,0:T(4,128)S(1)}, s32[]{:T(128)}, /*index=5*/s32[5]{0:T(128)S(1)}, s32[1]{0:T(128)}) while((s32[]{:T(128)}, f32[13,4,4,4,128]{4,3,2,1,0:T(4,128)S(1)}, s32[4,3]{1,0:T(4,128)}, f32[4,1,1,4,128]{4,3,2,1,0:T(4,128)S(1)}, ...), condition=%wide.while_cond.115, body=%wide.while_body.115.sunk | while | flops 1045 | bytes 6371 | solution.py:73
  2051.5 41.4 %while.168 = (s32[]{:T(128)}, f32[13,4,4,4,128]{4,3,2,1,0:T(4,128)S(1)}, s32[4,4]{1,0:T(4,128)}, f32[4,1,1,1,128]{4,3,2,1,0:T(1,128)S(1)}, s32[]{:T(128)}, /*index=5*/s32[5]{0:T(128)S(1)}, s32[1]{0:T(128)}, s32[]{:T(128)}) while((s32[]{:T(128)}, f32[13,4,4,4,128]{4,3,2,1,0:T(4,128)S(1)}, s32[4,4]{1,0:T(4,128)}, ...), condition=%wide.while_cond.116, body=%wide.while_body.116.sunk | while | flops 277 | bytes 2819 | solution.py:73
  2092.9 35.1 %while.169 = (s32[]{:T(128)}, f32[13,4,4,4,128]{4,3,2,1,0:T(4,128)S(1)}, s32[4,3]{1,0:T(4,128)}, f32[4,1,4,1,128]{4,3,2,1,0:T(1,128)S(1)}, s32[]{:T(128)}, /*index=5*/s32[5]{0:T(128)S(1)}, s32[1]{0:T(128)}, s32[]{:T(128)}) while((s32[]{:T(128)}, f32[13,4,4,4,128]{4,3,2,1,0:T(4,128)S(1)}, s32[4,3]{1,0:T(4,128)}, ...), condition=%wide.while_cond.117, body=%wide.while_body.117.sunk | while | flops 1045 | bytes 10479 | solution.py:73
  2128.0 18.6 while.170
  2146.6 34.6 %while.171 = (s32[]{:T(128)}, f32[13,4,4,4,128]{4,3,2,1,0:T(4,128)S(1)}, s32[4,3]{1,0:T(4,128)}, f32[4,1,4,1,128]{4,3,2,1,0:T(1,128)S(1)}, s32[]{:T(128)}, /*index=5*/s32[5]{0:T(128)S(1)}, s32[1]{0:T(128)}, s32[]{:T(128)}) while((s32[]{:T(128)}, f32[13,4,4,4,128]{4,3,2,1,0:T(4,128)S(1)}, s32[4,3]{1,0:T(4,128)}, ...), condition=%wide.while_cond.119, body=%wide.while_body.119.sunk | while | flops 1045 | bytes 10479 | solution.py:73
  2181.2 41.3 %while.172 = (s32[]{:T(128)}, f32[13,4,4,4,128]{4,3,2,1,0:T(4,128)S(1)}, s32[4,4]{1,0:T(4,128)}, f32[4,1,1,1,128]{4,3,2,1,0:T(1,128)S(1)}, s32[]{:T(128)}, /*index=5*/s32[5]{0:T(128)S(1)}, s32[1]{0:T(128)}, s32[]{:T(128)}) while((s32[]{:T(128)}, f32[13,4,4,4,128]{4,3,2,1,0:T(4,128)S(1)}, s32[4,4]{1,0:T(4,128)}, ...), condition=%wide.while_cond.120, body=%wide.while_body.120.sunk | while | flops 277 | bytes 2819 | solution.py:73
  2222.5 25.3 %while.173 = (s32[]{:T(128)}, f32[13,4,4,4,128]{4,3,2,1,0:T(4,128)S(1)}, s32[4,3]{1,0:T(4,128)}, f32[4,1,1,4,128]{4,3,2,1,0:T(4,128)S(1)}, s32[]{:T(128)}, /*index=5*/s32[5]{0:T(128)S(1)}, s32[1]{0:T(128)}) while((s32[]{:T(128)}, f32[13,4,4,4,128]{4,3,2,1,0:T(4,128)S(1)}, s32[4,3]{1,0:T(4,128)}, f32[4,1,1,4,128]{4,3,2,1,0:T(4,128)S(1)}, ...), condition=%wide.while_cond.121, body=%wide.while_body.121.sunk | while | flops 1045 | bytes 6371 | solution.py:73
  2247.9 40.2 %while.174 = (s32[]{:T(128)}, f32[13,4,4,4,128]{4,3,2,1,0:T(4,128)S(1)}, s32[4,4]{1,0:T(4,128)}, f32[4,1,1,1,128]{4,3,2,1,0:T(1,128)S(1)}, s32[]{:T(128)}, /*index=5*/s32[5]{0:T(128)S(1)}, s32[1]{0:T(128)}, s32[]{:T(128)}) while((s32[]{:T(128)}, f32[13,4,4,4,128]{4,3,2,1,0:T(4,128)S(1)}, s32[4,4]{1,0:T(4,128)}, ...), condition=%wide.while_cond.122, body=%wide.while_body.122.sunk | while | flops 277 | bytes 2819 | solution.py:73
  2296.1 4.8 collective-permute-start.15
  2309.1 122.2 %all-reduce.21.cloned.1.call-done = (f32[1,27,128,128]{3,2,1,0:T(8,128)}, f32[1,27,128,128]{3,2,1,0:T(8,128)}) async-done(((f32[1,27,128,128]{3,2,1,0:T(8,128)}, f32[1,27,128,128]{3,2,1,0:T(8,128)}), (f32[1,27,128,128]{3,2,1,0:T(8,128)}, f32[1,27,128,128]{3,2,1,0:T(8,128)})) %all-reduce.21.cloned.1.call-update) | async-done | bytes 3538960 | tf_op jit(solution)/shard_map/psum | solution.py:252
  2431.3 4.2 maximum_divide_fusion
  (1985 shorter events, 2067.9 us)
Async XLA Ops:
  7.2 253.3 %copy-start = (bf16[27,128,128]{2,1,0:T(8,128)(2,1)S(1)}, bf16[27,128,128]{2,1,0:T(8,128)(2,1)}, u32[]{:S(2)}) copy-start(bf16[27,128,128]{2,1,0:T(8,128)(2,1)} %param.170) | copy-start | bytes 2654212
  7.2 47.3 %copy-start.103 = (s32[5]{0:T(128)S(1)}, s32[5]{0:T(128)}, u32[]{:S(2)}) copy-start(s32[5]{0:T(128)} %constant.1912.clone.1) | copy-start | bytes 64
  7.2 43.3 %copy-start.98 = (f32[2,128]{1,0:T(2,128)S(1)}, f32[2,128]{1,0:T(2,128)}, u32[]{:S(2)}) copy-start(f32[2,128]{1,0:T(2,128)} %param.171) | copy-start | bytes 3076
  7.2 43.3 %copy-start.97 = (f32[2,128]{1,0:T(2,128)S(1)}, f32[2,128]{1,0:T(2,128)}, u32[]{:S(2)}) copy-start(f32[2,128]{1,0:T(2,128)} %param.172) | copy-start | bytes 3076
  7.2 2424.1 %all-reduce.21.cloned.1.call-start = ((), (), s32[]{:S(2)}) async-start(), calls=%async_computation | async-start | bytes 7077888 | tf_op jit(solution)/shard_map/psum | solution.py:252
  27.3 33.8 %collective-permute-start.1 = (bf16[3,4,4,4,128]{4,0,3,2,1:T(4,128)(2,1)S(1)}, bf16[3,4,4,4,128]{4,0,3,2,1:T(4,128)(2,1)S(1)}, u32[]{:S(2)}, u32[]{:S(2)}) collective-permute-start(bf16[3,4,4,4,128]{4,0,3,2,1:T(4,128)(2,1)S(1)} %pad_maximum_fusion.5), channel_id=1, source_target_pairs={{8,0},{16,8},{24,16},{9,1},{17,9},{25,17},{10,2},{18,10},{26,18},{... | collective-permute-start | bytes 147464 | tf_op jit(solution)/shard_map/ppermute | solution.py:13
  28.8 32.5 %collective-permute-start = (bf16[3,4,4,4,128]{4,0,3,2,1:T(4,128)(2,1)S(1)}, bf16[3,4,4,4,128]{4,0,3,2,1:T(4,128)(2,1)S(1)}, u32[]{:S(2)}, u32[]{:S(2)}) collective-permute-start(bf16[3,4,4,4,128]{4,0,3,2,1:T(4,128)(2,1)S(1)} %pad_maximum_fusion.4), channel_id=1, source_target_pairs={{0,8},{8,16},{16,24},{1,9},{9,17},{17,25},{2,10},{10,18},{18,26},{... | collective-permute-start | bytes 147464 | tf_op jit(solution)/shard_map/ppermute | solution.py:13
  36.6 39.8 %copy-start.68 = (pred[4]{0:T(512)(128)(4,1)}, pred[4]{0:T(512)(128)(4,1)S(1)}, u32[]{:S(2)}) copy-start(pred[4]{0:T(512)(128)(4,1)S(1)} %get-tuple-element.2452) | copy-start | bytes 16
  38.9 39.4 %copy-start.77 = (pred[4]{0:T(512)(128)(4,1)}, pred[4]{0:T(512)(128)(4,1)S(1)}, u32[]{:S(2)}) copy-start(pred[4]{0:T(512)(128)(4,1)S(1)} %get-tuple-element.2447) | copy-start | bytes 16
  39.0 40.0 %copy-start.65 = (pred[4]{0:T(512)(128)(4,1)}, pred[4]{0:T(512)(128)(4,1)S(1)}, u32[]{:S(2)}) copy-start(pred[4]{0:T(512)(128)(4,1)S(1)} %get-tuple-element.2445) | copy-start | bytes 16
  39.0 40.7 %copy-start.63 = (pred[4]{0:T(512)(128)(4,1)}, pred[4]{0:T(512)(128)(4,1)S(1)}, u32[]{:S(2)}) copy-start(pred[4]{0:T(512)(128)(4,1)S(1)} %get-tuple-element.2444) | copy-start | bytes 16
  39.0 42.1 %copy-start.76 = (pred[4]{0:T(512)(128)(4,1)}, pred[4]{0:T(512)(128)(4,1)S(1)}, u32[]{:S(2)}) copy-start(pred[4]{0:T(512)(128)(4,1)S(1)} %get-tuple-element.2443) | copy-start | bytes 16
  39.1 41.4 %copy-start.62 = (pred[4]{0:T(512)(128)(4,1)}, pred[4]{0:T(512)(128)(4,1)S(1)}, u32[]{:S(2)}) copy-start(pred[4]{0:T(512)(128)(4,1)S(1)} %get-tuple-element.2442) | copy-start | bytes 16
  39.1 42.7 %copy-start.75 = (pred[4]{0:T(512)(128)(4,1)}, pred[4]{0:T(512)(128)(4,1)S(1)}, u32[]{:S(2)}) copy-start(pred[4]{0:T(512)(128)(4,1)S(1)} %get-tuple-element.2441) | copy-start | bytes 16
  61.4 4.5 collective-permute-start.3
  62.9 3.9 collective-permute-start.2
  119.4 44.6 %copy-start.36 = (f32[128]{0:T(128)S(1)}, f32[128]{0:T(128)}, u32[]{:S(2)}) copy-start(f32[128]{0:T(128)} %get-tuple-element.2457) | copy-start | bytes 1540
  119.5 44.6 %copy-start.67 = (f32[128]{0:T(128)S(1)}, f32[128]{0:T(128)}, u32[]{:S(2)}) copy-start(f32[128]{0:T(128)} %get-tuple-element.2390) | copy-start | bytes 1540
  164.8 6.9 collective-permute-start.5
  166.9 6.7 collective-permute-start.4
  173.8 4.7 collective-permute-start.7
  175.2 3.9 collective-permute-start.6
  260.3 47.0 %copy-start.9 = (bf16[4,64,128]{2,1,0:T(8,128)(2,1)S(1)}, bf16[4,64,128]{2,1,0:T(8,128)(2,1)}, u32[]{:S(2)}) copy-start(bf16[4,64,128]{2,1,0:T(8,128)(2,1)} %param.168) | copy-start | bytes 196612
  260.3 47.0 %copy-start.27 = (bf16[4,64,128]{2,1,0:T(8,128)(2,1)S(1)}, bf16[4,64,128]{2,1,0:T(8,128)(2,1)}, u32[]{:S(2)}) copy-start(bf16[4,64,128]{2,1,0:T(8,128)(2,1)} %param.173) | copy-start | bytes 196612
  260.3 47.0 %copy-start.40 = (f32[128]{0:T(128)S(1)}, f32[128]{0:T(128)}, u32[]{:S(2)}) copy-start(f32[128]{0:T(128)} %get-tuple-element.2458) | copy-start | bytes 1540
  260.3 47.0 %copy-start.95 = (f32[128]{0:T(128)S(1)}, f32[128]{0:T(128)}, u32[]{:S(2)}) copy-start(f32[128]{0:T(128)} %get-tuple-element.2391) | copy-start | bytes 1540
  260.3 47.0 %copy-start.104 = (bf16[256]{0:T(256)(128)(2,1)S(1)}, bf16[256]{0:T(256)(128)(2,1)}, u32[]{:S(2)}) copy-start(bf16[256]{0:T(256)(128)(2,1)} %fusion.56) | copy-start | bytes 1540
  262.3 88.1 %copy-start.4 = (f32[256,128]{1,0:T(8,128)}, f32[256,128]{1,0:T(8,128)S(1)}, u32[]{:S(2)}) copy-start(f32[256,128]{1,0:T(8,128)S(1)} %get-tuple-element.2404) | copy-start | bytes 393220
  307.3 43.1 %copy-start.38 = (f32[128]{0:T(128)}, f32[128]{0:T(128)S(1)}, u32[]{:S(2)}) copy-start(f32[128]{0:T(128)S(1)} %get-tuple-element.1897) | copy-start | bytes 1540
  307.3 43.1 %copy-start.39 = (f32[128]{0:T(128)}, f32[128]{0:T(128)S(1)}, u32[]{:S(2)}) copy-start(f32[128]{0:T(128)S(1)} %get-tuple-element.1898) | copy-start | bytes 1540
  418.9 45.7 %copy-start.93 = (s32[4,3]{1,0:T(4,128)S(1)}, s32[4,3]{1,0:T(4,128)}, u32[]{:S(2)}) copy-start(s32[4,3]{1,0:T(4,128)} %concatenate.575) | copy-start | bytes 148
  419.0 45.7 %copy-start.108 = (s32[5]{0:T(128)S(1)}, s32[5]{0:T(128)}, u32[]{:S(2)}) copy-start(s32[5]{0:T(128)} %constant.3929) | copy-start | bytes 64
  419.0 71.7 %copy-start.86 = (s32[4,4]{1,0:T(4,128)S(1)}, s32[4,4]{1,0:T(4,128)}, u32[]{:S(2)}) copy-start(s32[4,4]{1,0:T(4,128)} %get-tuple-element.4726) | copy-start | bytes 196
  419.0 113.0 %copy-start.92 = (s32[4,3]{1,0:T(4,128)S(1)}, s32[4,3]{1,0:T(4,128)}, u32[]{:S(2)}) copy-start(s32[4,3]{1,0:T(4,128)} %concatenate.577) | copy-start | bytes 148
  419.0 113.0 %copy-start.111 = (s32[5]{0:T(128)S(1)}, s32[5]{0:T(128)}, u32[]{:S(2)}) copy-start(s32[5]{0:T(128)} %constant.3955) | copy-start | bytes 64
  423.2 143.1 %copy-start.23 = (s32[4,2]{0,1:T(2,128)S(1)}, s32[4,2]{0,1:T(2,128)}, u32[]{:S(2)}) copy-start(s32[4,2]{0,1:T(2,128)} %concatenate.578.clone) | copy-start | bytes 100
  423.2 283.9 %copy-start.85 = (s32[4,4]{1,0:T(4,128)S(1)}, s32[4,4]{1,0:T(4,128)}, u32[]{:S(2)}) copy-start(s32[4,4]{1,0:T(4,128)} %get-tuple-element.4864) | copy-start | bytes 196
  423.2 327.9 %copy-start.91 = (s32[4,3]{1,0:T(4,128)S(1)}, s32[4,3]{1,0:T(4,128)}, u32[]{:S(2)}) copy-start(s32[4,3]{1,0:T(4,128)} %concatenate.583) | copy-start | bytes 148
  423.3 364.4 %copy-start.22 = (s32[4,2]{0,1:T(2,128)S(1)}, s32[4,2]{0,1:T(2,128)}, u32[]{:S(2)}) copy-start(s32[4,2]{0,1:T(2,128)} %concatenate.584.clone) | copy-start | bytes 100
  566.2 312.0 %copy-start.5 = (f32[4,4,4,4,128]{4,3,2,1,0:T(4,128)S(1)}, f32[4,4,4,4,128]{4,3,2,1,0:T(4,128)}, u32[]{:S(2)}) copy-start(f32[4,4,4,4,128]{4,3,2,1,0:T(4,128)} %slice.5803) | copy-start | bytes 393220
  566.2 312.0 %copy-start.59 = (s32[4]{0:T(128)S(1)}, s32[4]{0:T(128)}, u32[]{:S(2)}) copy-start(s32[4]{0:T(128)} %get-tuple-element.1432) | copy-start | bytes 52
  629.0 279.4 %copy-start.94 = (s32[4,3]{1,0:T(4,128)S(1)}, s32[4,3]{1,0:T(4,128)}, u32[]{:S(2)}) copy-start(s32[4,3]{1,0:T(4,128)} %get-tuple-element.5005) | copy-start | bytes 148
  879.0 315.7 %copy-start.90 = (s32[4,3]{1,0:T(4,128)S(1)}, s32[4,3]{1,0:T(4,128)}, u32[]{:S(2)}) copy-start(s32[4,3]{1,0:T(4,128)} %concatenate.596) | copy-start | bytes 148
  879.0 352.5 %copy-start.84 = (s32[4,4]{1,0:T(4,128)S(1)}, s32[4,4]{1,0:T(4,128)}, u32[]{:S(2)}) copy-start(s32[4,4]{1,0:T(4,128)} %get-tuple-element.5212) | copy-start | bytes 196
  908.4 378.3 %copy-start.89 = (s32[4,3]{1,0:T(4,128)S(1)}, s32[4,3]{1,0:T(4,128)}, u32[]{:S(2)}) copy-start(s32[4,3]{1,0:T(4,128)} %concatenate.598) | copy-start | bytes 148
  945.2 367.8 %copy-start.83 = (s32[4,4]{1,0:T(4,128)S(1)}, s32[4,4]{1,0:T(4,128)}, u32[]{:S(2)}) copy-start(s32[4,4]{1,0:T(4,128)} %get-tuple-element.5257) | copy-start | bytes 196
  1087.2 199.5 %copy-start.109 = (s32[5]{0:T(128)S(1)}, s32[5]{0:T(128)}, u32[]{:S(2)}) copy-start(s32[5]{0:T(128)} %get-tuple-element.5364) | copy-start | bytes 64
  1286.7 85.3 %copy-start.26 = (f32[256]{0:T(256)S(1)}, f32[256]{0:T(256)}, u32[]{:S(2)}) copy-start(f32[256]{0:T(256)} %compare_convert_fusion) | copy-start | bytes 3076
  1286.7 85.3 %copy-start.33 = (f32[128]{0:T(128)S(1)}, f32[128]{0:T(128)}, u32[]{:S(2)}) copy-start(f32[128]{0:T(128)} %copy-done.32) | copy-start | bytes 1540
  1355.0 4.4 collective-permute-start.8
  1356.3 3.9 collective-permute-start.9
  1360.3 6.3 collective-permute-start.10
  1361.7 6.6 collective-permute-start.11
  1457.5 42.7 %copy-start.110 = (s32[5]{0:T(128)S(1)}, s32[5]{0:T(128)}, u32[]{:S(2)}) copy-start(s32[5]{0:T(128)} %get-tuple-element.5364) | copy-start | bytes 64
  1458.0 108.2 %copy-start.112 = (s32[5]{0:T(128)S(1)}, s32[5]{0:T(128)}, u32[]{:S(2)}) copy-start(s32[5]{0:T(128)} %get-tuple-element.5372) | copy-start | bytes 64
  1458.0 142.0 %copy-start.113 = (s32[5]{0:T(128)S(1)}, s32[5]{0:T(128)}, u32[]{:S(2)}) copy-start(s32[5]{0:T(128)} %get-tuple-element.5377) | copy-start | bytes 64
  1459.1 304.8 %copy-start.114 = (s32[5]{0:T(128)S(1)}, s32[5]{0:T(128)}, u32[]{:S(2)}) copy-start(s32[5]{0:T(128)} %get-tuple-element.5382) | copy-start | bytes 64
  1459.2 338.7 %copy-start.115 = (s32[5]{0:T(128)S(1)}, s32[5]{0:T(128)}, u32[]{:S(2)}) copy-start(s32[5]{0:T(128)} %get-tuple-element.5387) | copy-start | bytes 64
  1525.8 324.2 %copy-start.116 = (s32[5]{0:T(128)S(1)}, s32[5]{0:T(128)}, u32[]{:S(2)}) copy-start(s32[5]{0:T(128)} %get-tuple-element.5390) | copy-start | bytes 64
  1600.0 274.3 %copy-start.60 = (s32[4]{0:T(128)S(1)}, s32[4]{0:T(128)}, u32[]{:S(2)}) copy-start(s32[4]{0:T(128)} %get-tuple-element.1432) | copy-start | bytes 52
  2288.2 5.6 collective-permute-start.12
  2290.8 3.9 collective-permute-start.13
  2294.8 7.5 collective-permute-start.14
  2296.1 7.8 collective-permute-start.15
  (70 other events, 1091.5 us)
Sparse Core Ops, SparseCore 0:
  2289.7 141.5 all-reduce.20
where the time goes:
time: 2480 us; the launch traced here: 2440 us
  local copies, waits for them, and re-layouts  1100 us (44%)
  other arithmetic  938 us (38%)
  blocking collectives  172 us (7%)
  waiting for transfers between devices  130 us (5%)
  starting transfers between devices  42.7 us (2%)
  between operations  34.4 us (1%)
    scatter-add x768, local copies, waits for them, and re-layouts  946 us
    scatter-add x416, other arithmetic  797 us
    psum x1, waiting for transfers between devices, body(): dw_one, dw_two = lax.psum((dw_one, dw_two), ('gx', 'gy'))  122 us
    psum x2, blocking collectives, moments(): lax.psum((weighted, jnp.sum(values * occupied, axis=0), jnp.sum(values *...  87.1 us
    gather x54, local copies, waits for them, and re-layouts, assemble(): pieces.append(jnp.take(region, tile_table[:, d], axis=0))  61 us
  transfers between devices with their start and end apart: 17, of which 10 were waited for; matrix products, arithmetic and copies ran while one was open for 1% of the time, Pallas kernels for 0%

commit v1 on v0

v1 whole, which is shorter than its diff:
```python
import functools

import jax
import jax.numpy as jnp
import numpy as np
from jax import lax
from jax.experimental import pallas as pl
from jax.experimental.pallas import tpu as pltpu
from jax.sharding import PartitionSpec as P

MESH = pl.DeviceIdType.MESH
FACES = ((1, 0), (-1, 0), (0, 1), (0, -1))
CORNERS = ((1, 1), (1, -1), (-1, 1), (-1, -1))
epsilon = 1e-05
F32 = jnp.float32
BF16 = jnp.bfloat16


def plane_sources():
    direction = np.zeros((9, 16), np.int32)
    place = np.zeros((9, 16), np.int32)
    for s in range(9):
        for v in range(16):
            q, r = v // 4 + s // 3 - 1, v % 4 + s % 3 - 1
            oq, orr = (q >= 4) - (q < 0), (r >= 4) - (r < 0)
            direction[s, v] = 3 * (oq + 1) + orr + 1
            place[s, v] = 4 * (q - 4 * oq) + r - 4 * orr
    return direction.reshape(-1), place.reshape(-1)


def sigmoid(values):
    return 1.0 / (1.0 + jnp.exp(-values))


def slope(values):
    sigma = sigmoid(values)
    return sigma * (1.0 + values * (1.0 - sigma))


def dot(a, b, dims=((1,), (0,))):
    return lax.dot_general(a, b, (dims, ((), ())), preferred_element_type=F32)


def kernel(
    nx, ny, side, small,
    voxel_ref, w1_ref, w2_ref, gain_ref, shift_ref, grad_ref, count_ref, face_ref, corner_ref, rows_ref, cols_ref,
    out_ref, gin_ref, dw1_ref, dw2_ref, norms_ref,
    gather_ref, scatter_ref, mask_ref, fext_ref, zext_ref, zown_ref, eext_ref, q1_ref, q2_ref, d_ref,
    fsend_ref, zsend_ref, rsend_ref, ret_ref, xbuf_ref, ybuf_ref,
    halo_send, halo_recv, x_send, x_recv, y_send, y_recv,
):
    i, j = lax.axis_index("gx"), lax.axis_index("gy")
    bricks, _, _, channels = voxel_ref.shape
    entries = fext_ref.shape[0]
    vox = bricks * 64
    items = [(FACES[k], face_ref, k * side + t) for k in range(4) for t in range(side)]
    items += [(CORNERS[k], corner_ref, k * small + t) for k in range(4) for t in range(small)]

    def inside(dx, dy):
        ok = jnp.int32(1)
        if dx > 0:
            ok = ok * (i + 1 < nx).astype(jnp.int32)
        if dx < 0:
            ok = ok * (i > 0).astype(jnp.int32)
        if dy > 0:
            ok = ok * (j + 1 < ny).astype(jnp.int32)
        if dy < 0:
            ok = ok * (j > 0).astype(jnp.int32)
        return ok

    barrier = pltpu.get_barrier_semaphore()
    waits = jnp.int32(nx - 1 + ny - 1)
    for k in range(1, nx):
        pl.semaphore_signal(barrier, inc=1, device_id=(lax.rem(i + k, nx), j), device_id_type=MESH)
    for k in range(1, ny):
        pl.semaphore_signal(barrier, inc=1, device_id=(i, lax.rem(j + k, ny)), device_id_type=MESH)
    for dx, dy in CORNERS:
        there = inside(dx, dy)
        waits = waits + there

        @pl.when(there == 1)
        def _():
            pl.semaphore_signal(barrier, inc=1, device_id=(i + dx, j + dy), device_id_type=MESH)

    def halo(round_, n, src, dst, direction):
        dx, dy = direction
        return pltpu.make_async_remote_copy(
            src_ref=src, dst_ref=dst, send_sem=halo_send.at[round_, n], recv_sem=halo_recv.at[round_, n],
            device_id=(i + dx, j + dy), device_id_type=MESH,
        )

    def start_halo(round_, sources, targets, sign):
        for n, ((dx, dy), _, _) in enumerate(items):
            way = (sign * dx, sign * dy)

            @pl.when(inside(*way) == 1)
            def _():
                halo(round_, n, sources(n), targets(n), way).start()

    def end_halo(round_, sources, targets, sign):
        for n, ((dx, dy), _, _) in enumerate(items):
            way = (sign * dx, sign * dy)

            @pl.when(inside(-way[0], -way[1]) == 1)
            def _():
                halo(round_, n, sources(n), targets(n), (-way[0], -way[1])).wait_recv()

    def drain_halo(round_, sources, targets, sign):
        for n, ((dx, dy), _, _) in enumerate(items):
            way = (sign * dx, sign * dy)

            @pl.when(inside(*way) == 1)
            def _():
                halo(round_, n, sources(n), targets(n), way).wait_send()

    def x_copy(r, slot, k, to):
        return pltpu.make_async_remote_copy(
            src_ref=xbuf_ref.at[r, slot], dst_ref=xbuf_ref.at[r, slot], send_sem=x_send.at[r, k],
            recv_sem=x_recv.at[r, k], device_id=(to, j), device_id_type=MESH,
        )

    def y_copy(r, slot, k, to):
        return pltpu.make_async_remote_copy(
            src_ref=ybuf_ref.at[r, slot], dst_ref=ybuf_ref.at[r, slot], send_sem=y_send.at[r, k],
            recv_sem=y_recv.at[r, k], device_id=(i, to), device_id_type=MESH,
        )

    def start_sums(r, rows):
        slab = jnp.concatenate(rows + [jnp.zeros((8 - len(rows), channels), F32)], axis=0)
        xbuf_ref[r, i] = slab
        for k in range(1, nx):
            x_copy(r, i, k, lax.rem(i + k, nx)).start()

    def end_sums(r):
        for k in range(1, nx):
            x_copy(r, lax.rem(i - k + nx, nx), k, i).wait_recv()
        ybuf_ref[r, j] = jnp.sum(xbuf_ref[r], axis=0)
        for k in range(1, ny):
            y_copy(r, j, k, lax.rem(j + k, ny)).start()
        for k in range(1, ny):
            y_copy(r, lax.rem(j - k + ny, ny), k, j).wait_recv()
        return jnp.sum(ybuf_ref[r], axis=0)

    def drain_sums(r):
        for k in range(1, nx):
            x_copy(r, i, k, lax.rem(i + k, nx)).wait_send()
        for k in range(1, ny):
            y_copy(r, j, k, lax.rem(j + k, ny)).wait_send()

    def colsum(values):
        return jnp.sum(values, axis=0, keepdims=True)

    count = count_ref[0]
    entry = lax.broadcasted_iota(jnp.int32, mask_ref.shape, 0)
    mask = jnp.where(entry < count, 1.0, 0.0)
    mask = jnp.where(entry < bricks, mask, 0.0)
    for n, ((dx, dy), _, _) in enumerate(items):
        mask = jnp.where(entry == bricks + n, inside(-dx, -dy).astype(F32), mask)
    mask_ref[...] = mask
    fext_ref[:bricks] = (voxel_ref[...].astype(F32) * mask_ref[:bricks]).astype(BF16)
    for n, (_, list_ref, place) in enumerate(items):
        fsend_ref[n] = voxel_ref[list_ref[place]]
    pl.semaphore_wait(barrier, waits)
    features = (0, lambda n: fsend_ref.at[n], lambda n: fext_ref.at[bricks + n], 1)
    start_halo(*features)

    for o in range(3):
        lane = lax.broadcasted_iota(jnp.int32, gather_ref.shape[1:], 1)
        gather_ref[o] = jnp.where(lane == rows_ref[:, o : o + 1], 1.0, 0.0).astype(BF16)
        row = lax.broadcasted_iota(jnp.int32, scatter_ref.shape[1:], 0)
        scatter_ref[o] = jnp.where(row == cols_ref[o : o + 1, :], 1.0, 0.0).astype(BF16)

    def collect(field, q_ref):
        flat = [field[:, p].reshape(entries * 16, channels) for p in range(4)]
        low = dot(gather_ref[0], flat[3]).astype(BF16)
        mid = dot(gather_ref[1], jnp.concatenate(flat, axis=1)).astype(BF16)
        high = dot(gather_ref[2], flat[0]).astype(BF16)
        planes = [low] + [mid[:, p * channels : (p + 1) * channels] for p in range(4)] + [high]
        for a, plane in enumerate(planes):
            plane = plane.reshape(bricks, 9, 16, channels)
            for s in range(9):
                q_ref[:, a, :, s * channels : (s + 1) * channels] = plane[:, s]

    width = 9 * channels

    def taps(q_ref, a):
        return q_ref[:, a : a + 4].reshape(vox, width)

    def conv(q_ref, w_ref):
        total = dot(taps(q_ref, 0), w_ref[:width])
        for a in (1, 2):
            total = total + dot(taps(q_ref, a), w_ref[a * width : (a + 1) * width])
        return total

    def conv_weights(q_ref, grads, scale, dw_ref):
        for a in range(3):
            dw_ref[a * width : (a + 1) * width] = dot(taps(q_ref, a), grads, ((0,), (0,))) * scale

    def conv_back(grads, w_ref):
        parts = [
            dot(grads, w_ref[a * width : (a + 1) * width], ((1,), (1,))).reshape(bricks, 4, 16, width)
            for a in range(3)
        ]
        for a6 in range(6):
            piece = None
            for a in range(3):
                if 0 <= a6 - a < 4:
                    term = parts[a][:, a6 - a]
                    piece = term if piece is None else piece + term
            for s in range(9):
                d_ref[a6, :, s] = piece[:, :, s * channels : (s + 1) * channels]

        def spread(o, planes):
            value = [d_ref[a6].reshape(bricks * 144, channels) for a6 in planes]
            value = value[0] if len(value) == 1 else jnp.concatenate(value, axis=1)
            upper = value.astype(BF16)
            lower = (value - upper.astype(F32)).astype(BF16)
            return dot(scatter_ref[o], upper) + dot(scatter_ref[o], lower)

        mid = spread(1, (1, 2, 3, 4))
        low, high = spread(0, (0,)), spread(2, (5,))
        for p in range(4):
            value = mid[:, p * channels : (p + 1) * channels]
            if p == 3:
                value = value + low
            if p == 0:
                value = value + high
            eext_ref[:, p] = value.reshape(entries, 16, channels)

    def home(values):
        brick = lax.broadcasted_iota(jnp.int32, values.shape, 0)
        for n, ((dx, dy), list_ref, place) in enumerate(items):
            chosen = jnp.where(inside(dx, dy) == 1, list_ref[place], -1)
            values = values + jnp.where(brick == chosen, ret_ref[ret_base[0] + n].astype(F32)[None], 0.0)
        return values

    ret_base = [0]
    sent = len(items)

    end_halo(*features)
    fext_ref[bricks:] = jnp.where(mask_ref[bricks:] > 0.0, fext_ref[bricks:].astype(F32), 0.0).astype(BF16)
    collect(fext_ref, q1_ref)
    z1 = conv(q1_ref, w1_ref)
    zown_ref[...] = z1.reshape(bricks, 4, 16, channels)
    for n, (_, list_ref, place) in enumerate(items):
        zsend_ref[n] = zown_ref[list_ref[place]]
    raw = (1, lambda n: zsend_ref.at[n], lambda n: zext_ref.at[bricks + n], 1)
    occupied = mask_ref[:bricks].reshape(vox, channels)
    weighted = jnp.zeros((1, channels), F32) + 64.0 * count.astype(F32)
    start_sums(0, [colsum(z1 * occupied), colsum(z1 * z1 * occupied), weighted])
    start_halo(*raw)
    totals = end_sums(0)
    voxels = totals[2:3]
    mean1 = totals[0:1] / voxels
    recip1 = lax.rsqrt(totals[1:2] / voxels - mean1 * mean1 + epsilon)
    end_halo(*raw)

    gain1, gain2 = gain_ref[0:1], gain_ref[1:2]
    shift1, shift2 = shift_ref[0:1], shift_ref[1:2]
    wide = mask_ref[...].reshape(entries * 64, channels)
    zext_ref[:bricks] = zown_ref[...]
    zall = jnp.where(wide > 0.0, zext_ref[...].reshape(entries * 64, channels), 0.0)
    xh1 = (zall - mean1) * recip1
    zext_ref[...] = xh1.reshape(zext_ref.shape)
    u1 = gain1 * xh1 + shift1
    a1 = (u1 * sigmoid(u1) * wide).astype(BF16)
    collect(a1.reshape(entries, 4, 16, channels), q2_ref)
    z2 = conv(q2_ref, w2_ref)
    start_sums(1, [colsum(z2 * occupied), colsum(z2 * z2 * occupied)])
    totals = end_sums(1)
    mean2 = totals[0:1] / voxels
    recip2 = lax.rsqrt(totals[1:2] / voxels - mean2 * mean2 + epsilon)
    xh2 = (z2 - mean2) * recip2
    feats = fext_ref[:bricks].astype(F32).reshape(vox, channels)
    pre = gain2 * xh2 + shift2 + feats
    dv = grad_ref[...].astype(F32).reshape(vox, channels) * occupied * slope(pre)
    start_sums(2, [colsum(dv), colsum(dv * xh2)])
    out_ref[...] = (pre * sigmoid(pre) * occupied).astype(BF16).reshape(out_ref.shape)
    totals = end_sums(2)
    sd2, sx2 = totals[0:1], totals[1:2]
    dz2 = (occupied * gain2 * recip2 * (dv - sd2 / voxels - xh2 * (sx2 / voxels))).astype(BF16)
    root = lax.rsqrt(voxels)

    conv_back(dz2, w2_ref)
    rsend_ref[:sent] = eext_ref[bricks:].astype(BF16)
    back2 = (2, lambda n: rsend_ref.at[n], lambda n: ret_ref.at[n], -1)
    start_halo(*back2)
    xh1 = zext_ref[...].reshape(entries * 64, channels)
    part = eext_ref[...].reshape(entries * 64, channels) * wide * slope(gain1 * xh1 + shift1)
    start_sums(3, [colsum(part), colsum(part * xh1)])
    conv_weights(q2_ref, dz2, root, dw2_ref)
    totals = end_sums(3)
    sd1, sx1 = totals[0:1], totals[1:2]
    norms_ref[...] = jnp.concatenate([sx1, sd1, sx2, sd2], axis=0) * root
    end_halo(*back2)
    da1 = home(eext_ref[:bricks]).reshape(vox, channels)
    xh1 = zext_ref[:bricks].reshape(vox, channels)
    du1 = da1 * occupied * slope(gain1 * xh1 + shift1)
    dz1 = (occupied * gain1 * recip1 * (du1 - sd1 / voxels - xh1 * (sx1 / voxels))).astype(BF16)

    conv_back(dz1, w1_ref)
    rsend_ref[sent:] = eext_ref[bricks:].astype(BF16)
    back1 = (3, lambda n: rsend_ref.at[sent + n], lambda n: ret_ref.at[sent + n], -1)
    start_halo(*back1)
    conv_weights(q1_ref, dz1, root, dw1_ref)
    end_halo(*back1)
    ret_base[0] = sent
    back_in = home(eext_ref[:bricks]).reshape(vox, channels)
    gin_ref[...] = ((dv + back_in) * occupied).astype(BF16).reshape(gin_ref.shape)
    for way in (features, raw, back2, back1):
        drain_halo(*way)
    for r in range(4):
        drain_sums(r)


def solution(mesh):
    nx, ny = mesh.shape["gx"], mesh.shape["gy"]
    direction, place = plane_sources()

    def body(voxel, w1, w2, gain, shift, grad_out, brick_count, kernel_map, face_send, corner_send):
        bricks, _, channels = voxel.shape
        side, small = face_send.shape[2], corner_send.shape[2]
        sent = 4 * side + 4 * small
        entries = bricks + sent
        field = (bricks, 4, 16, channels)
        rows = bricks * 144
        targets = jnp.stack(
            [(kernel_map[:, 9 * o + direction] * 16 + place).reshape(rows) for o in range(3)], axis=0
        )
        vmem, smem = pl.BlockSpec(memory_space=pltpu.VMEM), pl.BlockSpec(memory_space=pltpu.SMEM)
        taps = w1.shape[0] * channels
        out, gin, dw1, dw2, norms = pl.pallas_call(
            functools.partial(kernel, nx, ny, side, small),
            out_shape=[
                jax.ShapeDtypeStruct(field, BF16),
                jax.ShapeDtypeStruct(field, BF16),
                jax.ShapeDtypeStruct((taps, channels), F32),
                jax.ShapeDtypeStruct((taps, channels), F32),
                jax.ShapeDtypeStruct((4, channels), F32),
            ],
            in_specs=[vmem] * 6 + [smem] * 3 + [vmem] * 2,
            out_specs=[vmem] * 5,
            scratch_shapes=[
                pltpu.VMEM((3, rows, entries * 16), BF16),
                pltpu.VMEM((3, entries * 16, rows), BF16),
                pltpu.VMEM((entries, 4, 16, channels), F32),
                pltpu.VMEM((entries, 4, 16, channels), BF16),
                pltpu.VMEM((entries, 4, 16, channels), F32),
                pltpu.VMEM((bricks, 4, 16, channels), F32),
                pltpu.VMEM((entries, 4, 16, channels), F32),
                pltpu.VMEM((bricks, 6, 16, 9 * channels), BF16),
                pltpu.VMEM((bricks, 6, 16, 9 * channels), BF16),
                pltpu.VMEM((6, bricks, 9, 16, channels), F32),
                pltpu.VMEM((sent, 4, 16, channels), BF16),
                pltpu.VMEM((sent, 4, 16, channels), F32),
                pltpu.VMEM((2 * sent, 4, 16, channels), BF16),
                pltpu.VMEM((2 * sent, 4, 16, channels), BF16),
                pltpu.VMEM((4, nx, 8, channels), F32),
                pltpu.VMEM((4, ny, 8, channels), F32),
                pltpu.SemaphoreType.DMA((4, sent)),
                pltpu.SemaphoreType.DMA((4, sent)),
                pltpu.SemaphoreType.DMA((4, nx)),
                pltpu.SemaphoreType.DMA((4, nx)),
                pltpu.SemaphoreType.DMA((4, ny)),
                pltpu.SemaphoreType.DMA((4, ny)),
            ],
            compiler_params=pltpu.CompilerParams(
                collective_id=0, has_side_effects=True, vmem_limit_bytes=50 * 1024 * 1024
            ),
        )(
            voxel.reshape(field), w1.reshape(taps, channels), w2.reshape(taps, channels), gain, shift,
            grad_out.reshape(field), brick_count, face_send.reshape(-1), corner_send.reshape(-1),
            targets.T, targets,
        )
        dw1, dw2 = lax.psum((dw1, dw2), ("gx", "gy"))
        weight_grads = jnp.stack([dw1, dw2]).reshape((2,) + w1.shape)
        return out.reshape(voxel.shape), gin.reshape(voxel.shape), weight_grads, norms

    tiles = P(("gx", "gy"))
    in_specs = (tiles, P(), P(), P(), P(), tiles, tiles, tiles, tiles, tiles)
    return jax.shard_map(
        body, mesh=mesh, in_specs=in_specs, out_specs=(tiles, tiles, P(), P()), check_vma=False
    )
```

time: 2480 us -> 223 us (0.09); the launches traced: 2440 us -> 223 us
  local copies, waits for them, and re-layouts: 1100 us -> 10.8 us
  other arithmetic: 938 us -> 7.05 us
  blocking collectives: 172 us -> 0 us
  Pallas kernels: 0 us -> 50.7 us
  starting transfers between devices: 42.7 us -> 0.04 us
    scatter-add x806 -> x0, local copies, waits for them, and re-layouts: 984 us -> none
    scatter-add x450 -> x0, other arithmetic: 820 us -> none
    psum x4 -> x0, blocking collectives: 172 us -> none  [the longest x2 87.1 us: moments(): lax.psum((weighted, jnp.sum(values * occupied, axis=0), jnp.sum(values *...]
    gather x54 -> x3, local copies, waits for them, and re-layouts: 61 us -> 1.99 us  [body(): kernel_map[:, 9 * o + direction] * 16 + place]
    pallas_call x0 -> x1, Pallas kernels: none -> 50.7 us  [body(): pl.pallas_call(functools.partial(kernel, nx, ny, side, small), out_shape=...]
    add x36 -> x1, other arithmetic: 45 us -> 0.76 us  [body(): kernel_map[:, 9 * o + direction] * 16 + place]
    ppermute x16 -> x0, starting transfers between devices: 42.7 us -> none  [shifted(): return lax.ppermute(value, axis, pairs)]
    select_n x73 -> x0, other arithmetic: 42.5 us -> none  [the longest x68 36.4 us: assemble(): pieces.append(jnp.take(region, tile_table[:, d], axis=0))]
  transfers between devices with their start and end apart: 17 -> 1, of which waited for: 10 -> 1; matrix products, arithmetic and copies ran while one was open for 1% -> 0% of each run, Pallas kernels for 0% -> 0%
where the time goes in v1:
time: 223 us
  waiting for transfers between devices  140 us (63%)
  Pallas kernels  50.7 us (23%)
  between operations  14.8 us (7%)
  local copies, waits for them, and re-layouts  10.8 us (5%)
  other arithmetic  7.05 us (3%)
    psum x1, waiting for transfers between devices, body(): dw1, dw2 = lax.psum((dw1, dw2), ('gx', 'gy'))  140 us
    pallas_call x1, Pallas kernels, body(): pl.pallas_call(functools.partial(kernel, nx, ny, side, small), out_shape=...  50.7 us
    unnamed x20, local copies, waits for them, and re-layouts  8.12 us
  transfers between devices with their start and end apart: 1, of which 1 were waited for; matrix products, arithmetic and copies ran while one was open for 0% of the time, Pallas kernels for 0%

profile of v1, /device:TPU:0, one launch (start us, length us, event | category | flops | bytes accessed | tf_op | source)
XLA Modules:
  0.0 222.9 jit_solution(3372029071141382016)
XLA Ops:
  7.2 0.0 copy-start
  7.2 0.0 all-reduce.3.cloned.1.call-start
  7.9 0.7 pad_clamp_fusion.2
  8.6 0.7 pad_clamp_fusion.1
  9.3 0.7 pad_clamp_fusion
  10.0 0.8 copy.21
  10.8 0.7 gather_fusion.2
  11.4 0.7 gather_fusion.1
  12.1 0.7 gather_fusion
  12.8 0.8 add_bitcast_fusion.2
  13.5 0.1 copy.22
  13.6 0.1 add.66
  13.7 0.1 copy.24
  13.8 0.1 add.69
  13.9 0.1 copy.26
  14.0 0.1 add.72
  14.1 0.2 copy.27.rows_ref
  14.2 0.0 copy-done
  14.3 0.0 copy-start.1
  14.3 1.2 copy-done.1
  15.4 0.0 copy-start.2
  15.4 0.8 copy-done.2
  16.3 0.0 copy-start.3
  16.3 0.8 copy-done.3
  17.1 0.0 copy-start.4
  17.1 0.7 copy-done.4
  17.8 0.0 copy-start.5
  17.8 0.7 copy-done.5
  18.5 0.0 copy-start.6
  18.5 0.7 copy-done.6
  19.1 0.0 copy-start.7
  19.1 0.7 copy-done.7
  19.8 50.7 %shard_map.192 = (bf16[4,4,16,128]{3,2,1,0:T(8,128)(2,1)S(1)}, bf16[4,4,16,128]{3,2,1,0:T(8,128)(2,1)S(1)}, f32[3456,128]{1,0:T(8,128)}, f32[3456,128]{1,0:T(8,128)}, f32[4,128]{1,0:T(4,128)S(1)}) custom-call(bf16[4,4,16,128]{3,2,1,0:T(8,128)(2,1)S(1)} %bitcast.20, bf16[3456,128]{1,0:T(8,128)(2,1)S(1)} %bitcast.18, bf16[3456,128]{1,0:T(8,128)(2,1)S(1)} %bitcast.19, ...), custom_call_target="tpu_custom_call" | custom-call | tf_op jit(solution)/shard_map/pallas_call | solution.py:332
  70.5 0.0 all-reduce.3.cloned.1.call-update
  70.5 139.6 %all-reduce.3.cloned.1.call-done = (f32[1,27,128,128]{3,2,1,0:T(8,128)}, f32[1,27,128,128]{3,2,1,0:T(8,128)}) async-done(((f32[1,27,128,128]{3,2,1,0:T(8,128)}, f32[1,27,128,128]{3,2,1,0:T(8,128)}), (f32[1,27,128,128]{3,2,1,0:T(8,128)}, f32[1,27,128,128]{3,2,1,0:T(8,128)})) %all-reduce.3.cloned.1.call-update) | async-done | bytes 3538960 | tf_op jit(solution)/shard_map/psum | solution.py:375
  210.1 4.2 %pad_maximum_fusion = f32[2,27,128,128]{3,2,1,0:T(8,128)} fusion(f32[1,27,128,128]{3,2,1,0:T(8,128)} %get-tuple-element.14, f32[1,27,128,128]{3,2,1,0:T(8,128)} %get-tuple-element.15), kind=kLoop, calls=%fused_computation.3 | loop fusion | flops 884736 | bytes 7077888 | tf_op jit(solution)/shard_map/stack | solution.py:376
  214.3 0.6 copy.34
  214.9 0.6 copy.35
  215.5 0.6 copy.36
  (1 shorter events, 0.0 us)
Async XLA Ops:
  7.2 7.1 %copy-start = (bf16[27,128,128]{2,1,0:T(8,128)(2,1)S(1)}, bf16[27,128,128]{2,1,0:T(8,128)(2,1)}, u32[]{:S(2)}) copy-start(bf16[27,128,128]{2,1,0:T(8,128)(2,1)} %param.18) | copy-start | bytes 2654212
  7.2 202.9 %all-reduce.3.cloned.1.call-start = ((), (), s32[]{:S(2)}) async-start(), calls=%async_computation | async-start | bytes 7077888 | tf_op jit(solution)/shard_map/psum | solution.py:375
  14.3 1.2 copy-start.1
  15.4 0.8 copy-start.2
  16.3 0.8 copy-start.3
  17.1 0.7 copy-start.4
  17.8 0.7 copy-start.5
  18.5 0.7 copy-start.6
  19.1 0.7 copy-start.7
Sparse Core Ops, SparseCore 0:
  70.6 139.3 all-reduce.2

commit v2 on v1

--- a/solution.py
+++ b/solution.py
@@ -2,7 +2,6 @@
 
 import jax
 import jax.numpy as jnp
-import numpy as np
 from jax import lax
 from jax.experimental import pallas as pl
 from jax.experimental.pallas import tpu as pltpu
@@ -16,16 +15,13 @@
 BF16 = jnp.bfloat16
 
 
-def plane_sources():
-    direction = np.zeros((9, 16), np.int32)
-    place = np.zeros((9, 16), np.int32)
-    for s in range(9):
-        for v in range(16):
-            q, r = v // 4 + s // 3 - 1, v % 4 + s % 3 - 1
-            oq, orr = (q >= 4) - (q < 0), (r >= 4) - (r < 0)
-            direction[s, v] = 3 * (oq + 1) + orr + 1
-            place[s, v] = 4 * (q - 4 * oq) + r - 4 * orr
-    return direction.reshape(-1), place.reshape(-1)
+def plane_sources(at):
+    s, q, r = at >> 4, (at >> 2) & 3, at & 3
+    tens = jnp.where(s >= 6, 2, jnp.where(s >= 3, 1, 0))
+    q, r = q + tens - 1, r + s - 3 * tens - 1
+    oq = jnp.where(q > 3, 1, jnp.where(q < 0, -1, 0))
+    orr = jnp.where(r > 3, 1, jnp.where(r < 0, -1, 0))
+    return 3 * (oq + 1) + orr + 1, 4 * (q - 4 * oq) + r - 4 * orr
 
 
 def sigmoid(values):
@@ -43,18 +39,21 @@
 
 def kernel(
     nx, ny, side, small,
-    voxel_ref, w1_ref, w2_ref, gain_ref, shift_ref, grad_ref, count_ref, face_ref, corner_ref, rows_ref, cols_ref,
-    out_ref, gin_ref, dw1_ref, dw2_ref, norms_ref,
+    voxel_ref, w1_hbm, w2_hbm, gain_ref, shift_ref, grad_hbm, count_ref, map_ref, face_ref, corner_ref,
+    out_ref, gin_ref, dw_ref, norms_ref,
+    w1_ref, w2_ref, grad_ref, load_sem,
     gather_ref, scatter_ref, mask_ref, fext_ref, zext_ref, zown_ref, eext_ref, q1_ref, q2_ref, d_ref,
     fsend_ref, zsend_ref, rsend_ref, ret_ref, xbuf_ref, ybuf_ref,
     halo_send, halo_recv, x_send, x_recv, y_send, y_recv,
+    part_ref, pair_ref, half_ref, cross_ref, quarter_ref, deep_ref, full_ref,
+    pair_send, pair_recv, cross_send, cross_recv, deep_send, deep_recv,
 ):
     i, j = lax.axis_index("gx"), lax.axis_index("gy")
     bricks, _, _, channels = voxel_ref.shape
     entries = fext_ref.shape[0]
     vox = bricks * 64
-    items = [(FACES[k], face_ref, k * side + t) for k in range(4) for t in range(side)]
-    items += [(CORNERS[k], corner_ref, k * small + t) for k in range(4) for t in range(small)]
+    items = [(FACES[k], face_ref, k, t) for k in range(4) for t in range(side)]
+    items += [(CORNERS[k], corner_ref, k, t) for k in range(4) for t in range(small)]
 
     def inside(dx, dy):
         ok = jnp.int32(1)
@@ -69,6 +68,12 @@
         return ok
 
     barrier = pltpu.get_barrier_semaphore()
+    loads = [
+        pltpu.make_async_copy(source, target, load_sem.at[n])
+        for n, (source, target) in enumerate([(w1_hbm, w1_ref), (w2_hbm, w2_ref), (grad_hbm, grad_ref)])
+    ]
+    for load in loads:
+        load.start()
     waits = jnp.int32(nx - 1 + ny - 1)
     for k in range(1, nx):
         pl.semaphore_signal(barrier, inc=1, device_id=(lax.rem(i + k, nx), j), device_id_type=MESH)
@@ -90,7 +95,7 @@
         )
 
     def start_halo(round_, sources, targets, sign):
-        for n, ((dx, dy), _, _) in enumerate(items):
+        for n, ((dx, dy), _, _, _) in enumerate(items):
             way = (sign * dx, sign * dy)
 
             @pl.when(inside(*way) == 1)
@@ -98,7 +103,7 @@
                 halo(round_, n, sources(n), targets(n), way).start()
 
     def end_halo(round_, sources, targets, sign):
-        for n, ((dx, dy), _, _) in enumerate(items):
+        for n, ((dx, dy), _, _, _) in enumerate(items):
             way = (sign * dx, sign * dy)
 
             @pl.when(inside(-way[0], -way[1]) == 1)
@@ -106,7 +111,7 @@
                 halo(round_, n, sources(n), targets(n), (-way[0], -way[1])).wait_recv()
 
     def drain_halo(round_, sources, targets, sign):
-        for n, ((dx, dy), _, _) in enumerate(items):
+        for n, ((dx, dy), _, _, _) in enumerate(items):
             way = (sign * dx, sign * dy)
 
             @pl.when(inside(*way) == 1)
@@ -154,21 +159,35 @@
     entry = lax.broadcasted_iota(jnp.int32, mask_ref.shape, 0)
     mask = jnp.where(entry < count, 1.0, 0.0)
     mask = jnp.where(entry < bricks, mask, 0.0)
-    for n, ((dx, dy), _, _) in enumerate(items):
+    for n, ((dx, dy), _, _, _) in enumerate(items):
         mask = jnp.where(entry == bricks + n, inside(-dx, -dy).astype(F32), mask)
     mask_ref[...] = mask
     fext_ref[:bricks] = (voxel_ref[...].astype(F32) * mask_ref[:bricks]).astype(BF16)
-    for n, (_, list_ref, place) in enumerate(items):
-        fsend_ref[n] = voxel_ref[list_ref[place]]
+    for n, (_, list_ref, k, t) in enumerate(items):
+        fsend_ref[n] = voxel_ref[list_ref[0, k, t]]
     pl.semaphore_wait(barrier, waits)
     features = (0, lambda n: fsend_ref.at[n], lambda n: fext_ref.at[bricks + n], 1)
     start_halo(*features)
 
+    lane = lax.broadcasted_iota(jnp.int32, (144, entries * 16), 1)
+    row = lax.broadcasted_iota(jnp.int32, scatter_ref.shape[1:], 0)
+    down, down_place = plane_sources(lax.broadcasted_iota(jnp.int32, (144, 1), 0))
+    across = lax.broadcasted_iota(jnp.int32, (1, bricks * 144), 1)
+    owner = jnp.zeros_like(across)
+    for b in range(1, bricks):
+        owner = owner + jnp.where(across >= b * 144, 1, 0)
+    along, along_place = plane_sources(across - 144 * owner)
+    along = along + 9 * owner
     for o in range(3):
-        lane = lax.broadcasted_iota(jnp.int32, gather_ref.shape[1:], 1)
-        gather_ref[o] = jnp.where(lane == rows_ref[:, o : o + 1], 1.0, 0.0).astype(BF16)
-        row = lax.broadcasted_iota(jnp.int32, scatter_ref.shape[1:], 0)
-        scatter_ref[o] = jnp.where(row == cols_ref[o : o + 1, :], 1.0, 0.0).astype(BF16)
+        tall = along_place
+        for b in range(bricks):
+            target = down_place
+            for d in range(9):
+                start = 16 * map_ref[b, 9 * o + d]
+                target = target + jnp.where(down == d, start, 0)
+                tall = tall + jnp.where(along == 9 * b + d, start, 0)
+            gather_ref[o, b * 144 : (b + 1) * 144] = jnp.where(lane == target, 1.0, 0.0).astype(BF16)
+        scatter_ref[o] = jnp.where(row == tall, 1.0, 0.0).astype(BF16)
 
     def collect(field, q_ref):
         flat = [field[:, p].reshape(entries * 16, channels) for p in range(4)]
@@ -192,9 +211,102 @@
             total = total + dot(taps(q_ref, a), w_ref[a * width : (a + 1) * width])
         return total
 
-    def conv_weights(q_ref, grads, scale, dw_ref):
+    def conv_weights(w, q_ref, grads, scale):
         for a in range(3):
-            dw_ref[a * width : (a + 1) * width] = dot(taps(q_ref, a), grads, ((0,), (0,))) * scale
+            value = dot(taps(q_ref, a), grads, ((0,), (0,))) * scale
+            part_ref[w, a * width : (a + 1) * width] = value.astype(BF16)
+        if part_ref.shape[1] > 3 * width:
+            part_ref[w, 3 * width :] = jnp.zeros((part_ref.shape[1] - 3 * width, channels), BF16)
+
+    nz = ny // 2
+    mate = lax.rem(j, 2)
+    level = j // 2
+    chunk = deep_ref.shape[2]
+    half = part_ref.shape[1] // 2
+
+    def pair_copy(w, way):
+        if way == 0:
+            source = part_ref.at[w, pl.ds(pl.multiple_of((1 - mate) * half, 16), half)]
+            target = pair_ref.at[w]
+        else:
+            source = target = full_ref.at[w, mate]
+        return pltpu.make_async_remote_copy(
+            src_ref=source, dst_ref=target, send_sem=pair_send.at[w, way], recv_sem=pair_recv.at[w, way],
+            device_id=(i, j + 1 - 2 * mate), device_id_type=MESH,
+        )
+
+    def pair_wait(w, way):
+        target = pair_ref.at[w] if way == 0 else full_ref.at[w, 1 - mate]
+        pltpu.make_async_remote_copy(
+            src_ref=target, dst_ref=target, send_sem=pair_send.at[w, way], recv_sem=pair_recv.at[w, way],
+            device_id=(i, j + 1 - 2 * mate), device_id_type=MESH,
+        ).wait_recv()
+
+    def cross_copy(w, way, k, receive):
+        to = lax.rem(i + k, nx)
+        slot = lax.rem(i - k + nx, nx) if receive else i
+        target = full_ref.at[w, mate, slot] if way else cross_ref.at[w, slot]
+        source = target if way or receive else half_ref.at[w, to]
+        return pltpu.make_async_remote_copy(
+            src_ref=source, dst_ref=target, send_sem=cross_send.at[w, way, k], recv_sem=cross_recv.at[w, way, k],
+            device_id=(to, j), device_id_type=MESH,
+        )
+
+    def deep_copy(w, way, k, receive):
+        to = lax.rem(level + k, nz)
+        slot = lax.rem(level - k + nz, nz) if receive else level
+        target = full_ref.at[w, mate, i, slot] if way else deep_ref.at[w, slot]
+        source = target if way or receive else quarter_ref.at[w, to]
+        return pltpu.make_async_remote_copy(
+            src_ref=source, dst_ref=target, send_sem=deep_send.at[w, way, k], recv_sem=deep_recv.at[w, way, k],
+            device_id=(i, 2 * to + mate), device_id_type=MESH,
+        )
+
+    def reduce_step(w, step):
+        if step == 0:
+            pair_copy(w, 0).start()
+        if step == 1:
+            pair_wait(w, 0)
+            own = part_ref[w, pl.ds(pl.multiple_of(mate * half, 16), half)]
+            value = own.astype(F32) + pair_ref[w].astype(F32)
+            half_ref[w] = value.astype(BF16).reshape(half_ref.shape[1:])
+            for k in range(1, nx):
+                cross_copy(w, 0, k, False).start()
+            cross_ref[w, i] = half_ref[w, i]
+        if step == 2:
+            for k in range(1, nx):
+                cross_copy(w, 0, k, True).wait_recv()
+            value = jnp.sum(cross_ref[w].astype(F32), axis=0)
+            quarter_ref[w] = value.astype(BF16).reshape(quarter_ref.shape[1:])
+            for k in range(1, nz):
+                deep_copy(w, 0, k, False).start()
+            deep_ref[w, level] = quarter_ref[w, level]
+        if step == 3:
+            for k in range(1, nz):
+                deep_copy(w, 0, k, True).wait_recv()
+            full_ref[w, mate, i, level] = jnp.sum(deep_ref[w].astype(F32), axis=0).astype(BF16)
+            for k in range(1, nz):
+                deep_copy(w, 1, k, False).start()
+        if step == 4:
+            for k in range(1, nz):
+                deep_copy(w, 1, k, True).wait_recv()
+            for k in range(1, nx):
+                cross_copy(w, 1, k, False).start()
+        if step == 5:
+            for k in range(1, nx):
+                cross_copy(w, 1, k, True).wait_recv()
+            pair_copy(w, 1).start()
+        if step == 6:
+            pair_wait(w, 1)
+            dw_ref[w] = full_ref[w].reshape(dw_ref.shape[1:])
+
+    def drain_reduce(w):
+        for way in range(2):
+            pair_copy(w, way).wait_send()
+            for k in range(1, nx):
+                cross_copy(w, way, k, False).wait_send()
+            for k in range(1, nz):
+                deep_copy(w, way, k, False).wait_send()
 
     def conv_back(grads, w_ref):
         parts = [
@@ -229,8 +341,8 @@
 
     def home(values):
         brick = lax.broadcasted_iota(jnp.int32, values.shape, 0)
-        for n, ((dx, dy), list_ref, place) in enumerate(items):
-            chosen = jnp.where(inside(dx, dy) == 1, list_ref[place], -1)
+        for n, ((dx, dy), list_ref, k, t) in enumerate(items):
+            chosen = jnp.where(inside(dx, dy) == 1, list_ref[0, k, t], -1)
             values = values + jnp.where(brick == chosen, ret_ref[ret_base[0] + n].astype(F32)[None], 0.0)
         return values
 
@@ -240,10 +352,11 @@
     end_halo(*features)
     fext_ref[bricks:] = jnp.where(mask_ref[bricks:] > 0.0, fext_ref[bricks:].astype(F32), 0.0).astype(BF16)
     collect(fext_ref, q1_ref)
+    loads[0].wait()
     z1 = conv(q1_ref, w1_ref)
     zown_ref[...] = z1.reshape(bricks, 4, 16, channels)
-    for n, (_, list_ref, place) in enumerate(items):
-        zsend_ref[n] = zown_ref[list_ref[place]]
+    for n, (_, list_ref, k, t) in enumerate(items):
+        zsend_ref[n] = zown_ref[list_ref[0, k, t]]
     raw = (1, lambda n: zsend_ref.at[n], lambda n: zext_ref.at[bricks + n], 1)
     occupied = mask_ref[:bricks].reshape(vox, channels)
     weighted = jnp.zeros((1, channels), F32) + 64.0 * count.astype(F32)
@@ -265,6 +378,7 @@
     u1 = gain1 * xh1 + shift1
     a1 = (u1 * sigmoid(u1) * wide).astype(BF16)
     collect(a1.reshape(entries, 4, 16, channels), q2_ref)
+    loads[1].wait()
     z2 = conv(q2_ref, w2_ref)
     start_sums(1, [colsum(z2 * occupied), colsum(z2 * z2 * occupied)])
     totals = end_sums(1)
@@ -273,6 +387,7 @@
     xh2 = (z2 - mean2) * recip2
     feats = fext_ref[:bricks].astype(F32).reshape(vox, channels)
     pre = gain2 * xh2 + shift2 + feats
+    loads[2].wait()
     dv = grad_ref[...].astype(F32).reshape(vox, channels) * occupied * slope(pre)
     start_sums(2, [colsum(dv), colsum(dv * xh2)])
     out_ref[...] = (pre * sigmoid(pre) * occupied).astype(BF16).reshape(out_ref.shape)
@@ -288,8 +403,10 @@
     xh1 = zext_ref[...].reshape(entries * 64, channels)
     part = eext_ref[...].reshape(entries * 64, channels) * wide * slope(gain1 * xh1 + shift1)
     start_sums(3, [colsum(part), colsum(part * xh1)])
-    conv_weights(q2_ref, dz2, root, dw2_ref)
+    conv_weights(1, q2_ref, dz2, root)
+    reduce_step(1, 0)
     totals = end_sums(3)
+    reduce_step(1, 1)
     sd1, sx1 = totals[0:1], totals[1:2]
     norms_ref[...] = jnp.concatenate([sx1, sd1, sx2, sd2], axis=0) * root
     end_halo(*back2)
@@ -302,11 +419,22 @@
     rsend_ref[sent:] = eext_ref[bricks:].astype(BF16)
     back1 = (3, lambda n: rsend_ref.at[sent + n], lambda n: ret_ref.at[sent + n], -1)
     start_halo(*back1)
-    conv_weights(q1_ref, dz1, root, dw1_ref)
+    reduce_step(1, 2)
+    conv_weights(0, q1_ref, dz1, root)
+    reduce_step(0, 0)
+    reduce_step(1, 3)
+    reduce_step(0, 1)
     end_halo(*back1)
     ret_base[0] = sent
     back_in = home(eext_ref[:bricks]).reshape(vox, channels)
     gin_ref[...] = ((dv + back_in) * occupied).astype(BF16).reshape(gin_ref.shape)
+    for step in (4, 5, 6):
+        reduce_step(1, step)
+        reduce_step(0, step - 2)
+    for step in (5, 6):
+        reduce_step(0, step)
+    for w in range(2):
+        drain_reduce(w)
     for way in (features, raw, back2, back1):
         drain_halo(*way)
     for r in range(4):
@@ -315,7 +443,6 @@
 
 def solution(mesh):
     nx, ny = mesh.shape["gx"], mesh.shape["gy"]
-    direction, place = plane_sources()
 
     def body(voxel, w1, w2, gain, shift, grad_out, brick_count, kernel_map, face_send, corner_send):
         bricks, _, channels = voxel.shape
@@ -324,23 +451,27 @@
         entries = bricks + sent
         field = (bricks, 4, 16, channels)
         rows = bricks * 144
-        targets = jnp.stack(
-            [(kernel_map[:, 9 * o + direction] * 16 + place).reshape(rows) for o in range(3)], axis=0
-        )
+        parts = 2 * nx * (ny // 2)
+        chunk = -(-w1.shape[0] * channels // (16 * parts)) * 16
         vmem, smem = pl.BlockSpec(memory_space=pltpu.VMEM), pl.BlockSpec(memory_space=pltpu.SMEM)
+        hbm = pl.BlockSpec(memory_space=pl.ANY)
+        nz = ny // 2
         taps = w1.shape[0] * channels
-        out, gin, dw1, dw2, norms = pl.pallas_call(
+        out, gin, dw, norms = pl.pallas_call(
             functools.partial(kernel, nx, ny, side, small),
             out_shape=[
                 jax.ShapeDtypeStruct(field, BF16),
                 jax.ShapeDtypeStruct(field, BF16),
-                jax.ShapeDtypeStruct((taps, channels), F32),
-                jax.ShapeDtypeStruct((taps, channels), F32),
+                jax.ShapeDtypeStruct((2, parts * chunk, channels), BF16),
                 jax.ShapeDtypeStruct((4, channels), F32),
             ],
-            in_specs=[vmem] * 6 + [smem] * 3 + [vmem] * 2,
-            out_specs=[vmem] * 5,
+            in_specs=[vmem, hbm, hbm, vmem, vmem, hbm] + [smem] * 4,
+            out_specs=[vmem] * 4,
             scratch_shapes=[
+                pltpu.VMEM((taps, channels), BF16),
+                pltpu.VMEM((taps, channels), BF16),
+                pltpu.VMEM(field, BF16),
+                pltpu.SemaphoreType.DMA((3,)),
                 pltpu.VMEM((3, rows, entries * 16), BF16),
                 pltpu.VMEM((3, entries * 16, rows), BF16),
                 pltpu.VMEM((entries, 4, 16, channels), F32),
@@ -363,17 +494,28 @@
                 pltpu.SemaphoreType.DMA((4, nx)),
                 pltpu.SemaphoreType.DMA((4, ny)),
                 pltpu.SemaphoreType.DMA((4, ny)),
+                pltpu.VMEM((2, parts * chunk, channels), BF16),
+                pltpu.VMEM((2, parts * chunk // 2, channels), BF16),
+                pltpu.VMEM((2, nx, nz * chunk, channels), BF16),
+                pltpu.VMEM((2, nx, nz * chunk, channels), BF16),
+                pltpu.VMEM((2, nz, chunk, channels), BF16),
+                pltpu.VMEM((2, nz, chunk, channels), BF16),
+                pltpu.VMEM((2, 2, nx, nz, chunk, channels), BF16),
+                pltpu.SemaphoreType.DMA((2, 2)),
+                pltpu.SemaphoreType.DMA((2, 2)),
+                pltpu.SemaphoreType.DMA((2, 2, nx)),
+                pltpu.SemaphoreType.DMA((2, 2, nx)),
+                pltpu.SemaphoreType.DMA((2, 2, nz)),
+                pltpu.SemaphoreType.DMA((2, 2, nz)),
             ],
             compiler_params=pltpu.CompilerParams(
-                collective_id=0, has_side_effects=True, vmem_limit_bytes=50 * 1024 * 1024
+                collective_id=0, has_side_effects=True, vmem_limit_bytes=56 * 1024 * 1024
             ),
         )(
             voxel.reshape(field), w1.reshape(taps, channels), w2.reshape(taps, channels), gain, shift,
-            grad_out.reshape(field), brick_count, face_send.reshape(-1), corner_send.reshape(-1),
-            targets.T, targets,
-        )
-        dw1, dw2 = lax.psum((dw1, dw2), ("gx", "gy"))
-        weight_grads = jnp.stack([dw1, dw2]).reshape((2,) + w1.shape)
+            grad_out.reshape(field), brick_count, kernel_map, face_send, corner_send,
+        )
+        weight_grads = dw[:, :taps].astype(F32).reshape((2,) + w1.shape)
         return out.reshape(voxel.shape), gin.reshape(voxel.shape), weight_grads, norms
 
     tiles = P(("gx", "gy"))

time: 223 us -> 91.6 us (0.41)
  waiting for transfers between devices: 140 us -> 0 us
  Pallas kernels: 50.7 us -> 81.8 us
  between operations: 14.8 us -> 1.32 us
  other arithmetic: 7.05 us -> 2.21 us
  local copies, waits for them, and re-layouts: 10.8 us -> 6.07 us
    psum x1 -> x0, waiting for transfers between devices: 140 us -> none  [body(): dw1, dw2 = lax.psum((dw1, dw2), ('gx', 'gy'))]
    pallas_call x1, Pallas kernels: 50.7 us -> 81.8 us  [body(): pl.pallas_call(functools.partial(kernel, nx, ny, side, small), out_shape=...]
    another operation x2 -> x0, other arithmetic: 4.23 us -> none  [the longest x1 4.21 us: body(): weight_grads = jnp.stack([dw1, dw2]).reshape((2,) + w1.shape)]
    unnamed x20 -> x11, local copies, waits for them, and re-layouts: 8.12 us -> 4.47 us
  transfers between devices with their start and end apart: 1 -> 0, of which waited for: 1 -> 0; matrix products, arithmetic and copies ran while one was open for 0% -> 0% of each run, Pallas kernels for 0% -> 0%
where the time goes in v2:
time: 91.6 us; the launch traced here: 91.4 us
  Pallas kernels  81.8 us (89%)
  local copies, waits for them, and re-layouts  6.07 us (7%)
  other arithmetic  2.21 us (2%)
  between operations  1.32 us (1%)
    pallas_call x1, Pallas kernels, body(): pl.pallas_call(functools.partial(kernel, nx, ny, side, small), out_shape=...  81.8 us
    unnamed x11, local copies, waits for them, and re-layouts  4.47 us
    reshape x1, other arithmetic, body(): weight_grads = dw[:, :taps].astype(F32).reshape((2,) + w1.shape)  2.21 us

profile of v2, /device:TPU:0, one launch (start us, length us, event | category | flops | bytes accessed | tf_op | source)
XLA Modules:
  0.0 91.4 jit_solution(12060729779464987023)
XLA Ops:
  1.3 1.3 %copy.14.face_ref = s32[1,4,1]{2,1,0:T(4,128)} copy(s32[1,4,1]{1,2,0:T(1,128)} %param.18) | data formatting | bytes 32 | tf_op args[8]
  2.6 1.3 %copy.15.corner_ref = s32[1,4,1]{2,1,0:T(4,128)} copy(s32[1,4,1]{1,2,0:T(1,128)} %param.19) | data formatting | bytes 32 | tf_op args[9]
  3.9 81.8 %shard_map.129 = (bf16[4,4,16,128]{3,2,1,0:T(8,128)(2,1)}, bf16[4,4,16,128]{3,2,1,0:T(8,128)(2,1)}, bf16[2,3584,128]{2,1,0:T(8,128)(2,1)}, f32[4,128]{1,0:T(4,128)}) custom-call(bf16[4,4,16,128]{3,2,1,0:T(8,128)(2,1)} %bitcast.11, bf16[3456,128]{1,0:T(8,128)(2,1)} %bitcast.9, bf16[3456,128]{1,0:T(8,128)(2,1)} %bitcast.10, f32[2,128]{1,0:T(2,128)} %gain_ref.1, ...), custom_call_target="tpu_custom_call" | custom-call | tf_op jit(solution)/shard_map/pallas_call | solution.py:460
  85.7 1.6 %slice.3 = bf16[2,3456,128]{2,1,0:T(8,128)(2,1)S(1)} slice(bf16[2,3584,128]{2,1,0:T(8,128)(2,1)} %get-tuple-element.10), slice={[0:2], [0:3456], [0:128]} | slice | bytes 3538944 | tf_op jit(solution)/shard_map/slice | solution.py:518
  87.3 0.0 copy-start.1
  87.3 0.0 copy-start
  87.3 0.0 copy-start.2
  87.3 2.2 %convert.1 = f32[2,27,128,128]{3,2,1,0:T(8,128)} convert(bf16[2,27,128,128]{3,2,1,0:T(8,128)(2,1)S(1)} %bitcast.8) | non-fusion elementwise | flops 884736 | bytes 5308416 | tf_op jit(solution)/shard_map/reshape | solution.py:518
  89.6 0.0 copy-done.1
  89.6 0.6 copy.20
  90.2 0.0 copy-done
  90.2 0.6 copy.21
  90.8 0.0 copy-done.2
  90.8 0.6 copy.22
Async XLA Ops:
  87.3 2.2 %copy-start.1 = (bf16[4,4,16,128]{3,2,1,0:T(8,128)(2,1)S(1)}, bf16[4,4,16,128]{3,2,1,0:T(8,128)(2,1)}, u32[]{:S(2)}) copy-start(bf16[4,4,16,128]{3,2,1,0:T(8,128)(2,1)} %get-tuple-element.8) | copy-start | bytes 196612
  87.3 2.9 %copy-start = (bf16[4,4,16,128]{3,2,1,0:T(8,128)(2,1)S(1)}, bf16[4,4,16,128]{3,2,1,0:T(8,128)(2,1)}, u32[]{:S(2)}) copy-start(bf16[4,4,16,128]{3,2,1,0:T(8,128)(2,1)} %get-tuple-element.9) | copy-start | bytes 196612
  87.3 3.5 %copy-start.2 = (f32[4,128]{1,0:T(4,128)S(1)}, f32[4,128]{1,0:T(4,128)}, u32[]{:S(2)}) copy-start(f32[4,128]{1,0:T(4,128)} %get-tuple-element.19) | copy-start | bytes 6148

commit v3 on v2

--- a/solution.py
+++ b/solution.py
@@ -52,8 +52,8 @@
     bricks, _, _, channels = voxel_ref.shape
     entries = fext_ref.shape[0]
     vox = bricks * 64
-    items = [(FACES[k], face_ref, k, t) for k in range(4) for t in range(side)]
-    items += [(CORNERS[k], corner_ref, k, t) for k in range(4) for t in range(small)]
+    items = [(FACES[k], face_ref, k * side + t) for k in range(4) for t in range(side)]
+    items += [(CORNERS[k], corner_ref, k * small + t) for k in range(4) for t in range(small)]
 
     def inside(dx, dy):
         ok = jnp.int32(1)
@@ -95,7 +95,7 @@
         )
 
     def start_halo(round_, sources, targets, sign):
-        for n, ((dx, dy), _, _, _) in enumerate(items):
+        for n, ((dx, dy), _, _) in enumerate(items):
             way = (sign * dx, sign * dy)
 
             @pl.when(inside(*way) == 1)
@@ -103,7 +103,7 @@
                 halo(round_, n, sources(n), targets(n), way).start()
 
     def end_halo(round_, sources, targets, sign):
-        for n, ((dx, dy), _, _, _) in enumerate(items):
+        for n, ((dx, dy), _, _) in enumerate(items):
             way = (sign * dx, sign * dy)
 
             @pl.when(inside(-way[0], -way[1]) == 1)
@@ -111,7 +111,7 @@
                 halo(round_, n, sources(n), targets(n), (-way[0], -way[1])).wait_recv()
 
     def drain_halo(round_, sources, targets, sign):
-        for n, ((dx, dy), _, _, _) in enumerate(items):
+        for n, ((dx, dy), _, _) in enumerate(items):
             way = (sign * dx, sign * dy)
 
             @pl.when(inside(*way) == 1)
@@ -136,12 +136,16 @@
         for k in range(1, nx):
             x_copy(r, i, k, lax.rem(i + k, nx)).start()
 
-    def end_sums(r):
+    def turn_sums(r):
         for k in range(1, nx):
             x_copy(r, lax.rem(i - k + nx, nx), k, i).wait_recv()
         ybuf_ref[r, j] = jnp.sum(xbuf_ref[r], axis=0)
         for k in range(1, ny):
             y_copy(r, j, k, lax.rem(j + k, ny)).start()
+
+    def end_sums(r, turned=False):
+        if not turned:
+            turn_sums(r)
         for k in range(1, ny):
             y_copy(r, lax.rem(j - k + ny, ny), k, j).wait_recv()
         return jnp.sum(ybuf_ref[r], axis=0)
@@ -159,12 +163,12 @@
     entry = lax.broadcasted_iota(jnp.int32, mask_ref.shape, 0)
     mask = jnp.where(entry < count, 1.0, 0.0)
     mask = jnp.where(entry < bricks, mask, 0.0)
-    for n, ((dx, dy), _, _, _) in enumerate(items):
+    for n, ((dx, dy), _, _) in enumerate(items):
         mask = jnp.where(entry == bricks + n, inside(-dx, -dy).astype(F32), mask)
     mask_ref[...] = mask
     fext_ref[:bricks] = (voxel_ref[...].astype(F32) * mask_ref[:bricks]).astype(BF16)
-    for n, (_, list_ref, k, t) in enumerate(items):
-        fsend_ref[n] = voxel_ref[list_ref[0, k, t]]
+    for n, (_, list_ref, place) in enumerate(items):
+        fsend_ref[n] = voxel_ref[list_ref[place]]
     pl.semaphore_wait(barrier, waits)
     features = (0, lambda n: fsend_ref.at[n], lambda n: fext_ref.at[bricks + n], 1)
     start_halo(*features)
@@ -211,11 +215,11 @@
             total = total + dot(taps(q_ref, a), w_ref[a * width : (a + 1) * width])
         return total
 
-    def conv_weights(w, q_ref, grads, scale):
-        for a in range(3):
+    def conv_weights(w, q_ref, grads, scale, planes=(0, 1, 2)):
+        for a in planes:
             value = dot(taps(q_ref, a), grads, ((0,), (0,))) * scale
             part_ref[w, a * width : (a + 1) * width] = value.astype(BF16)
-        if part_ref.shape[1] > 3 * width:
+        if 2 in planes and part_ref.shape[1] > 3 * width:
             part_ref[w, 3 * width :] = jnp.zeros((part_ref.shape[1] - 3 * width, channels), BF16)
 
     nz = ny // 2
@@ -298,7 +302,7 @@
             pair_copy(w, 1).start()
         if step == 6:
             pair_wait(w, 1)
-            dw_ref[w] = full_ref[w].reshape(dw_ref.shape[1:])
+            dw_ref[w] = full_ref[w].reshape(part_ref.shape[1:])[: 3 * width]
 
     def drain_reduce(w):
         for way in range(2):
@@ -341,8 +345,8 @@
 
     def home(values):
         brick = lax.broadcasted_iota(jnp.int32, values.shape, 0)
-        for n, ((dx, dy), list_ref, k, t) in enumerate(items):
-            chosen = jnp.where(inside(dx, dy) == 1, list_ref[0, k, t], -1)
+        for n, ((dx, dy), list_ref, place) in enumerate(items):
+            chosen = jnp.where(inside(dx, dy) == 1, list_ref[place], -1)
             values = values + jnp.where(brick == chosen, ret_ref[ret_base[0] + n].astype(F32)[None], 0.0)
         return values
 
@@ -355,8 +359,8 @@
     loads[0].wait()
     z1 = conv(q1_ref, w1_ref)
     zown_ref[...] = z1.reshape(bricks, 4, 16, channels)
-    for n, (_, list_ref, k, t) in enumerate(items):
-        zsend_ref[n] = zown_ref[list_ref[0, k, t]]
+    for n, (_, list_ref, place) in enumerate(items):
+        zsend_ref[n] = zown_ref[list_ref[place]]
     raw = (1, lambda n: zsend_ref.at[n], lambda n: zext_ref.at[bricks + n], 1)
     occupied = mask_ref[:bricks].reshape(vox, channels)
     weighted = jnp.zeros((1, channels), F32) + 64.0 * count.astype(F32)
@@ -403,9 +407,11 @@
     xh1 = zext_ref[...].reshape(entries * 64, channels)
     part = eext_ref[...].reshape(entries * 64, channels) * wide * slope(gain1 * xh1 + shift1)
     start_sums(3, [colsum(part), colsum(part * xh1)])
-    conv_weights(1, q2_ref, dz2, root)
+    conv_weights(1, q2_ref, dz2, root, (0,))
+    turn_sums(3)
+    conv_weights(1, q2_ref, dz2, root, (1, 2))
     reduce_step(1, 0)
-    totals = end_sums(3)
+    totals = end_sums(3, True)
     reduce_step(1, 1)
     sd1, sx1 = totals[0:1], totals[1:2]
     norms_ref[...] = jnp.concatenate([sx1, sd1, sx2, sd2], axis=0) * root
@@ -415,22 +421,24 @@
     du1 = da1 * occupied * slope(gain1 * xh1 + shift1)
     dz1 = (occupied * gain1 * recip1 * (du1 - sd1 / voxels - xh1 * (sx1 / voxels))).astype(BF16)
 
+    conv_weights(0, q1_ref, dz1, root)
+    reduce_step(0, 0)
+    reduce_step(1, 2)
+    reduce_step(0, 1)
     conv_back(dz1, w1_ref)
     rsend_ref[sent:] = eext_ref[bricks:].astype(BF16)
     back1 = (3, lambda n: rsend_ref.at[sent + n], lambda n: ret_ref.at[sent + n], -1)
     start_halo(*back1)
-    reduce_step(1, 2)
-    conv_weights(0, q1_ref, dz1, root)
-    reduce_step(0, 0)
     reduce_step(1, 3)
-    reduce_step(0, 1)
+    reduce_step(0, 2)
+    reduce_step(1, 4)
     end_halo(*back1)
     ret_base[0] = sent
     back_in = home(eext_ref[:bricks]).reshape(vox, channels)
     gin_ref[...] = ((dv + back_in) * occupied).astype(BF16).reshape(gin_ref.shape)
-    for step in (4, 5, 6):
-        reduce_step(1, step)
-        reduce_step(0, step - 2)
+    for step in (3, 4):
+        reduce_step(0, step)
+        reduce_step(1, step + 2)
     for step in (5, 6):
         reduce_step(0, step)
     for w in range(2):
@@ -462,7 +470,7 @@
             out_shape=[
                 jax.ShapeDtypeStruct(field, BF16),
                 jax.ShapeDtypeStruct(field, BF16),
-                jax.ShapeDtypeStruct((2, parts * chunk, channels), BF16),
+                jax.ShapeDtypeStruct((2, taps, channels), BF16),
                 jax.ShapeDtypeStruct((4, channels), F32),
             ],
             in_specs=[vmem, hbm, hbm, vmem, vmem, hbm] + [smem] * 4,
@@ -513,9 +521,9 @@
             ),
         )(
             voxel.reshape(field), w1.reshape(taps, channels), w2.reshape(taps, channels), gain, shift,
-            grad_out.reshape(field), brick_count, kernel_map, face_send, corner_send,
-        )
-        weight_grads = dw[:, :taps].astype(F32).reshape((2,) + w1.shape)
+            grad_out.reshape(field), brick_count, kernel_map, face_send.reshape(-1), corner_send.reshape(-1),
+        )
+        weight_grads = dw.astype(F32).reshape((2,) + w1.shape)
         return out.reshape(voxel.shape), gin.reshape(voxel.shape), weight_grads, norms
 
     tiles = P(("gx", "gy"))

time: 91.6 us -> 82.9 us (0.905)
  Pallas kernels: 81.8 us -> 75.8 us
  local copies, waits for them, and re-layouts: 6.07 us -> 1.85 us
  other arithmetic: 2.21 us -> 3.73 us
    pallas_call x1, Pallas kernels: 81.8 us -> 75.8 us  [body(): pl.pallas_call(functools.partial(kernel, nx, ny, side, small), out_shape=...]
    unnamed x11 -> x9, local copies, waits for them, and re-layouts: 4.47 us -> 1.85 us
    slice x1 -> x0, local copies, waits for them, and re-layouts: 1.6 us -> none  [body(): weight_grads = dw[:, :taps].astype(F32).reshape((2,) + w1.shape)]
    reshape x1, other arithmetic: 2.21 us -> 3.73 us  [body(): weight_grads = dw.astype(F32).reshape((2,) + w1.shape)]
where the time goes in v3:
time: 82.9 us; the launch traced here: 82.7 us
  Pallas kernels  75.8 us (91%)
  other arithmetic  3.73 us (4%)
  local copies, waits for them, and re-layouts  1.85 us (2%)
  between operations  1.31 us (2%)
    pallas_call x1, Pallas kernels, body(): pl.pallas_call(functools.partial(kernel, nx, ny, side, small), out_shape=...  75.8 us
    reshape x1, other arithmetic, body(): weight_grads = dw.astype(F32).reshape((2,) + w1.shape)  3.73 us
    unnamed x9, local copies, waits for them, and re-layouts  1.85 us

profile of v3, /device:TPU:0, one launch (start us, length us, event | category | flops | bytes accessed | tf_op | source)
XLA Modules:
  0.0 82.7 jit_solution(9534743897722006550)
XLA Ops:
  1.3 75.8 %shard_map.129 = (bf16[4,4,16,128]{3,2,1,0:T(8,128)(2,1)}, bf16[4,4,16,128]{3,2,1,0:T(8,128)(2,1)}, bf16[2,3456,128]{2,1,0:T(8,128)(2,1)}, f32[4,128]{1,0:T(4,128)}) custom-call(bf16[4,4,16,128]{3,2,1,0:T(8,128)(2,1)} %bitcast.13, bf16[3456,128]{1,0:T(8,128)(2,1)} %bitcast.11, bf16[3456,128]{1,0:T(8,128)(2,1)} %bitcast.12, f32[2,128]{1,0:T(2,128)} %gain_ref.1, ...), custom_call_target="tpu_custom_call" | custom-call | tf_op jit(solution)/shard_map/pallas_call | solution.py:468
  77.1 0.0 copy-start.1
  77.1 0.0 copy-start
  77.1 0.0 copy-start.2
  77.1 3.7 %convert.1 = f32[2,27,128,128]{3,2,1,0:T(8,128)} convert(bf16[2,27,128,128]{3,2,1,0:T(8,128)(2,1)} %bitcast.10) | non-fusion elementwise | flops 884736 | bytes 5308416 | tf_op jit(solution)/shard_map/reshape | solution.py:526
  80.9 0.0 copy-done.1
  80.9 0.6 copy.18
  81.5 0.0 copy-done
  81.5 0.6 copy.19
  82.1 0.0 copy-done.2
  82.1 0.6 copy.20
Async XLA Ops:
  77.1 3.8 %copy-start.1 = (bf16[4,4,16,128]{3,2,1,0:T(8,128)(2,1)S(1)}, bf16[4,4,16,128]{3,2,1,0:T(8,128)(2,1)}, u32[]{:S(2)}) copy-start(bf16[4,4,16,128]{3,2,1,0:T(8,128)(2,1)} %get-tuple-element.8) | copy-start | bytes 196612
  77.1 4.4 %copy-start = (bf16[4,4,16,128]{3,2,1,0:T(8,128)(2,1)S(1)}, bf16[4,4,16,128]{3,2,1,0:T(8,128)(2,1)}, u32[]{:S(2)}) copy-start(bf16[4,4,16,128]{3,2,1,0:T(8,128)(2,1)} %get-tuple-element.9) | copy-start | bytes 196612
  77.1 5.0 %copy-start.2 = (f32[4,128]{1,0:T(4,128)S(1)}, f32[4,128]{1,0:T(4,128)}, u32[]{:S(2)}) copy-start(f32[4,128]{1,0:T(4,128)} %get-tuple-element.19) | copy-start | bytes 6148
